TPU v7x, 128 devices: a whole 4x4x4 slice. The times are simulated.
128 devices in a mesh: stn: 8 (over x_lo, y), src: 16 (over z, x_hi, core).
Axes of the slice: x: 4 (x_hi: 2, x_lo: 2; x = x_hi * 2 + x_lo), y: 4, z: 4, core: 2. Of those that a mesh axis runs over, the one named last changes fastest.
Arguments:
- beam_jones: bfloat16 [8, 512, 16384], P(None, 'stn', 'src'), may hold values from -3 to 3
- source_lm: float32 [2, 16384], P(None, 'src'), may hold values from -0.3 to 0.3
- source_flux: float32 [16384], P('src'), may hold values from 0.3 to 3
- live_counts: int32 [16], P('src'), may hold values from 1 to 1024, 9216 in all
- station_uvw: float32 [3, 512], replicated, may hold values from -400 to 400
- chan_scale: float32 [4], replicated, may hold values from 0.9 to 1.1
- block_pairs: int32 [136, 2], P('stn'), may hold values from 0 to 15, as said below
Outputs:
- visibility: float32 [136, 32768], P('stn', 'src')
Inputs may be any that keep to these rules, and one draw needn't show every extreme that they name: `block_pairs`: each row holds two station blocks i <= j; every such pair of the 16 blocks appears exactly once. `live_counts`: some shard is full (1024 live); the counts sum to 9216.
All inputs are finite; a program needn't handle non-finite values.
Results may differ from a plain program's by a relative error of at most 0.00081.
Values may be sent and summed in bfloat16 or wider, within the bound.
No kernel may reach another device: no remote copies, remote signals or barrier semaphores. Data moves between devices by JAX's collectives and lax.ppermute only.
A program may use at most 128 MiB of HBM per device.

v0:
```python
import functools
import math

import jax
import jax.numpy as jnp
import numpy as np
from jax import lax
from jax.experimental import pallas as pl
from jax.experimental.pallas import tpu as pltpu
from jax.sharding import PartitionSpec as P

NBLK = 16
STN = 8
PAIRS_DEV = 17
LANES = 128
JROWS = 512
EXTRA = 16
ROWS = JROWS + EXTRA
OUT_ROWS = PAIRS_DEV * 16
KCOL = 512
ACC = (2560, 256)

TWO_PI_HI = 6.28125
TWO_PI_LO = 2.0 * math.pi - 6.28125
def _fit(fun, power, terms):
    x = np.cos(np.pi * (np.arange(4000) + 0.5) / 4000) * (math.pi * 1.001)
    cols = np.stack([x ** (2 * n + power) for n in range(terms)], 1)
    scale = np.abs(cols).max(0)
    sol, *_ = np.linalg.lstsq(cols / scale, fun(x), rcond=None)
    return [float(v) for v in sol / scale]


SIN_TERMS = _fit(np.sin, 1, 7)
COS_TERMS = _fit(np.cos, 0, 8)


def horner(square, terms):
    total = jnp.full_like(square, terms[-1])
    for term in terms[-2::-1]:
        total = total * square + term
    return total


def three(rows, at):
    return (rows[at : at + 1] + rows[at + 1 : at + 2]) + rows[at + 2 : at + 3]


def split3(x):
    first = x.astype(jnp.bfloat16).astype(jnp.float32)
    second = (x - first).astype(jnp.bfloat16).astype(jnp.float32)
    return [first, second, x - first - second]


def prep_kernel(live_ref, lm_hbm, flux_hbm, pairs_hbm, jones_hbm, out_ref, *refs):
    lm_ref, flux_ref, pairs_ref, jones_ref, info_ref, sems = refs
    copies = [
        pltpu.make_async_copy(src, dst, sems.at[n])
        for n, (src, dst) in enumerate(
            ((jones_hbm, jones_ref), (lm_hbm, lm_ref), (flux_hbm, flux_ref), (pairs_hbm, pairs_ref))
        )
    ]
    for copy in copies:
        copy.start()
    for copy in copies[1:]:
        copy.wait()
    slots = jones_ref.shape[2]
    dir_l, dir_m = lm_ref[0:1, :], lm_ref[1:2, :]
    live = (lax.broadcasted_iota(jnp.int32, (1, slots), 1) < live_ref[0]).astype(jnp.float32)
    amp = jnp.sqrt(flux_ref[...] * live * (1.0 / math.sqrt(slots * 16)))
    depth = jnp.sqrt(1.0 - dir_l * dir_l - dir_m * dir_m) - 1.0
    info_ref[...] = jnp.zeros_like(info_ref)
    for n, row in enumerate((dir_l, dir_m, depth, amp)):
        for t, term in enumerate(split3(row)):
            info_ref[3 * n + t : 3 * n + t + 1, :] = term
    for d in range(STN):
        info_ref[12:14, LANES * d : LANES * d + PAIRS_DEV] = pairs_ref[...].astype(jnp.float32)
    copies[0].wait()
    src = lax.axis_index("src")
    first = 2 * (src // 4) + src % 2
    for d in range(STN):
        cols = pl.ds(pl.multiple_of((d + first) % STN * LANES, LANES), LANES)
        for comp in range(8):
            out_ref[d, 64 * comp : 64 * comp + 64, :] = jones_ref[comp, :, cols]
        out_ref[d, JROWS:ROWS, :] = info_ref[:, cols].astype(jnp.bfloat16)


def acc_at(tile, part):
    return 256 * (tile * (tile + 1) // 2) + 128 * (tile + 1) * part


def gram_piece(step, l_ref, g_ref, before_ref, acc_ref):
    tile, part = 3 - step // 2, step % 2
    rows = 128 * (tile + 1)
    at = acc_at(tile, part)
    got = lax.dot_general(
        l_ref[512 * part : 512 * part + rows, :], g_ref[256 * tile : 256 * tile + 256, :],
        (((1,), (1,)), ((), ())), preferred_element_type=jnp.float32,
    )
    acc_ref[at : at + rows, :] = got if before_ref is None else before_ref[at : at + rows, :] + got


def field_piece(stn, held, uvw_ref, scale, kappa, g_ref, l_ref):
    ref, at = (held[0], stn) if len(held) == 1 else (held[stn // 4], stn % 4)
    info = ref[0, JROWS:ROWS, :].astype(jnp.float32)
    dir_l, dir_m, depth, amp = (three(info, 3 * n) for n in range(4))
    for odd in range(2):
        blk = 2 * stn + odd
        here = slice(32 * blk, 32 * blk + 32)
        geometry = (uvw_ref[0, here, :] * dir_l + uvw_ref[1, here, :] * dir_m) + uvw_ref[2, here, :] * depth
        phase = scale * geometry
        turns = jnp.round(phase * (0.5 / math.pi))
        angle = (phase - turns * TWO_PI_HI) - turns * TWO_PI_LO
        square = angle * angle
        sine = horner(square, SIN_TERMS) * (angle * amp)
        cosine = horner(square, COS_TERMS) * amp
        for a in range(2):
            g_rows = slice(64 * blk + 32 * a, 64 * blk + 32 * a + 32)
            own = pl.ds(pl.multiple_of(64 * blk + 32 * a + 16 * kappa, 16), 16)
            l_re = slice(32 * blk + 16 * a, 32 * blk + 16 * a + 16)
            l_im = slice(512 + 32 * blk + 16 * a, 512 + 32 * blk + 16 * a + 16)
            for k in range(2):
                row = 64 * (2 * a + k) + 32 * odd
                real = ref[at, row : row + 32, :].astype(jnp.float32)
                imag = ref[at, 256 + row : 288 + row, :].astype(jnp.float32)
                c_re = slice(2 * k * LANES, (2 * k + 1) * LANES)
                c_im = slice((2 * k + 1) * LANES, (2 * k + 2) * LANES)
                g_ref[g_rows, c_re] = (real * cosine + imag * sine).astype(jnp.bfloat16)
                g_ref[g_rows, c_im] = (imag * cosine - real * sine).astype(jnp.bfloat16)
                x_re = g_ref[own, c_re]
                x_im = g_ref[own, c_im]
                l_ref[l_re, c_re] = x_re
                l_ref[l_re, c_im] = x_im
                l_ref[l_im, c_re] = x_im
                l_ref[l_im, c_im] = -x_re


def pack_pairs(acc_ref, idx_ref, out_ref):
    low = lax.broadcasted_iota(jnp.int32, (16, LANES), 1) < 64
    for i in range(NBLK):
        for tile in range(i // 2, NBLK // 2):
            cols = slice(LANES * (tile % 2), LANES * (tile % 2) + LANES)
            for part in range(2):
                top = acc_at(tile // 2, part) + 32 * i
                row0 = acc_ref[top : top + 16, cols]
                row1 = acc_ref[top + 16 : top + 32, cols]
                at = (part * NBLK + i) * NBLK + 2 * tile
                if i <= 2 * tile:
                    even = jnp.where(low, row0, pltpu.roll(row1, 64, 1))
                    out_ref[idx_ref[at]] = even.astype(out_ref.dtype)
                odd = jnp.where(low, pltpu.roll(row0, 64, 1), row1)
                out_ref[idx_ref[at + 1]] = odd.astype(out_ref.dtype)


def slab_kernel(chan, packs, chained, counts, *refs):
    scal_ref, int_ref, *refs = refs
    idx_ref = refs.pop(0) if packs else None
    uvw_ref, *refs = refs
    sets, source_refs = len(counts), []
    for count in counts:
        source_refs.append(refs[:count])
        refs = refs[count:]
    before_ref = refs.pop(0) if chained else None
    out_refs, refs = (refs[:4], refs[4:]) if packs else (refs[:1], refs[1:])
    acc_ref, held_ref, sems = refs[4:] if packs else (out_refs[0], None, None)
    work = (refs[0:2], refs[2:4])
    scale, kappa = scal_ref[chan], int_ref[0]
    for n in range(sets + 1):
        for step in range(STN):
            if n < sets:
                field_piece(step, source_refs[n], uvw_ref, scale, kappa, *work[n % 2])
            if n > 0:
                g_ref, l_ref = work[(n - 1) % 2]
                gram_piece(step, l_ref, g_ref, acc_ref if n > 1 else before_ref, acc_ref)
    if packs:
        pack_pairs(acc_ref, idx_ref, held_ref)
        each = 4 * PAIRS_DEV
        copies = [
            pltpu.make_async_copy(held_ref.at[each * n : each * n + each], out_ref, sems.at[n])
            for n, out_ref in enumerate(out_refs)
        ]
        for copy in copies:
            copy.start()
        for copy in copies:
            copy.wait()


def add_far_kernel(one, two, three, four, real_ref, imag_ref):
    total = one[...].astype(jnp.float32)
    for ref in (two, three, four):
        total = total + ref[...].astype(jnp.float32)
    real_ref[...] = total[: 2 * PAIRS_DEV]
    imag_ref[...] = total[2 * PAIRS_DEV :].astype(imag_ref.dtype)


def add_near_kernel(int_ref, one, two, three, four, real_ref, imag_ref, *outs):
    for n, out_ref in enumerate(outs):
        rows = slice(PAIRS_DEV * n, PAIRS_DEV * n + PAIRS_DEV)
        total = one[rows].astype(jnp.float32)
        for ref in (two, three, four):
            total = total + ref[rows].astype(jnp.float32)
        x_to = (int_ref[1] + n) % 4
        there = pl.ds(x_to % 2 * PAIRS_DEV, PAIRS_DEV)
        far = jnp.where(x_to < 2, real_ref[there], imag_ref[there].astype(jnp.float32))
        out_ref[...] = (total + far).reshape(out_ref.shape)


def sum_kernel(*refs):
    shares, (order_ref, out_ref, held_ref) = refs[:-3], refs[-3:]
    total = shares[0][...]
    for ref in shares[1:]:
        total = total + ref[...]
    held_ref[...] = jnp.dot(
        total, order_ref[...], precision=lax.Precision.HIGHEST, preferred_element_type=jnp.float32
    )
    for st in range(16):
        out_ref[:, LANES * st : LANES * st + LANES] = held_ref[pl.ds(st, PAIRS_DEV, stride=16), :]


VMEM = pl.BlockSpec(memory_space=pltpu.VMEM)
SMEM = pl.BlockSpec(memory_space=pltpu.SMEM)
PARAMS = pltpu.CompilerParams(vmem_limit_bytes=14 * 1024 * 1024)
ALONE = pltpu.CompilerParams(vmem_limit_bytes=62 * 1024 * 1024)
WORK = [pltpu.VMEM((1024, KCOL), jnp.bfloat16)] * 4
SEND = jnp.bfloat16


def coords():
    return [(xl, y, z, xh, core) for xl in range(2) for y in range(4) for z in range(4) for xh in range(2) for core in range(2)]


def place_of(xl, y, z, xh, core):
    return (xl * 4 + y % 4) * 16 + (z % 4) * 4 + xh * 2 + core


def move(x, dx=0, dy=0, dz=0, dcore=0, apart=0):
    perm = []
    for xl, y, z, xh, core in coords():
        x_to = (2 * xh + xl + dx) % 4
        z_to = z + dz + (apart if core == 0 else -apart)
        perm.append((place_of(xl, y, z, xh, core), place_of(x_to % 2, y + dy, z_to, x_to // 2, core ^ dcore)))
    return lax.ppermute(x, ("stn", "src"), perm)


def body(beam_jones, source_lm, source_flux, live_counts, station_uvw, chan_scale, block_pairs):
    src, stn = lax.axis_index("src"), lax.axis_index("stn")
    plane = src // 4
    x_own, y_own = 2 * ((src // 2) % 2) + stn // 4, stn % 4
    ints = jnp.stack([src % 2, x_own]).astype(jnp.int32)
    message = pl.pallas_call(
        prep_kernel,
        out_shape=jax.ShapeDtypeStruct((STN, ROWS, LANES), jnp.bfloat16),
        in_specs=[SMEM] + [pl.BlockSpec(memory_space=pl.ANY)] * 4,
        out_specs=VMEM,
        scratch_shapes=[
            pltpu.VMEM((2, STN * LANES), jnp.float32),
            pltpu.VMEM((1, STN * LANES), jnp.float32),
            pltpu.VMEM((2, PAIRS_DEV), jnp.int32),
            pltpu.VMEM((8, 64, STN * LANES), jnp.bfloat16),
            pltpu.VMEM((EXTRA, STN * LANES), jnp.float32),
            pltpu.SemaphoreType.DMA((4,)),
        ],
        compiler_params=ALONE,
    )(live_counts, source_lm, source_flux.reshape(1, -1), block_pairs.T, beam_jones)

    own = lax.all_to_all(message, "stn", 0, 0, tiled=True)
    got = [move(own[:4], apart=1), move(own[4:], apart=1)]
    other = move(own, dcore=1)

    listed = other[:, JROWS + 12 : JROWS + 14, :PAIRS_DEV].astype(jnp.int32)
    holder = jnp.repeat(jnp.arange(STN, dtype=jnp.int32), PAIRS_DEV)
    slot = jnp.tile(jnp.arange(PAIRS_DEV, dtype=jnp.int32), STN)
    key = (listed[:, 0] * NBLK + listed[:, 1]).reshape(1, -1)
    hit = key == jnp.arange(NBLK * NBLK, dtype=jnp.int32)[:, None]
    part = jnp.arange(2, dtype=jnp.int32)[:, None]
    dy, dx = (holder % 4 - y_own) % 4, (2 * part + holder // 4 - x_own) % 4
    place = jnp.stack([dy * 4 + dx, dy * 4 + 2 * part + holder // 4]) * PAIRS_DEV + slot
    index = jnp.sum(jnp.where(hit[None, None], place[:, :, None, :], 0), axis=3).reshape(2, -1)

    scale = (2.0 * math.pi * chan_scale)[jnp.stack([plane, (plane + 2) % 4])]
    uvw = jnp.broadcast_to(station_uvw[:, :, None], (3, station_uvw.shape[1], LANES))

    square = jax.ShapeDtypeStruct(ACC, jnp.float32)
    packed = [jax.ShapeDtypeStruct((4 * PAIRS_DEV, 16, LANES), SEND)] * 4

    def slab(chan, packs, sources, before=None):
        chained = before is not None
        flat = [x for held in sources for x in held]
        return pl.pallas_call(
            functools.partial(slab_kernel, chan, packs, chained, [len(x) for x in sources]),
            out_shape=packed if packs else square,
            in_specs=[SMEM] * (3 if packs else 2) + [VMEM] * (1 + len(flat) + chained),
            out_specs=[pl.BlockSpec(memory_space=pl.ANY)] * 4 if packs else VMEM,
            scratch_shapes=WORK + ([
                pltpu.VMEM(ACC, jnp.float32), pltpu.VMEM((16 * PAIRS_DEV, 16, LANES), SEND), pltpu.SemaphoreType.DMA((4,))
            ] if packs else []),
            input_output_aliases={3 + len(flat): 0} if chained and not packs else {},
            compiler_params=PARAMS,
        )(scale, ints, *([index[chan]] if packs else []), uvw, *flat, *([before] if chained else []))

    def along_y(shares):
        return [shares[0]] + [move(shares[n], dy=n) for n in (1, 2, 3)]

    far = slab(1, False, [[own], [other]])
    near = slab(0, False, [[own], [other]])
    near, far, *got = lax.optimization_barrier((near, far, *got))
    other = [move(x, dcore=1) for x in got]
    far = slab(1, False, [got], far)
    far, *other = lax.optimization_barrier((far, *other))
    far = slab(1, True, [other], far)
    near, *far = lax.optimization_barrier((near, *far))
    near = slab(0, True, [got, other], near)
    small = jax.ShapeDtypeStruct((OUT_ROWS, LANES), jnp.float32)
    real, imag = pl.pallas_call(
        add_far_kernel,
        out_shape=[jax.ShapeDtypeStruct((2 * PAIRS_DEV, 16, LANES), t) for t in (jnp.float32, SEND)],
        in_specs=[VMEM] * 4, out_specs=[VMEM] * 2, compiler_params=PARAMS,
    )(*along_y(far))
    near = pl.pallas_call(
        add_near_kernel, out_shape=[small] * 4, in_specs=[SMEM] + [VMEM] * 6, out_specs=[VMEM] * 4,
        compiler_params=PARAMS,
    )(ints, *along_y(near), move(real, dz=2), move(imag, dz=2))
    near = [near[0]] + [move(near[n], dx=n) for n in (1, 2, 3)]

    lane = np.arange(LANES)
    order = np.zeros((LANES, LANES), np.float32)
    order[lane, (lane // 64) * 64 + (lane % 32) * 2 + (lane // 32) % 2] = 1.0
    return pl.pallas_call(
        sum_kernel,
        out_shape=jax.ShapeDtypeStruct((PAIRS_DEV, 2048), jnp.float32),
        in_specs=[VMEM] * 5,
        out_specs=VMEM,
        scratch_shapes=[pltpu.VMEM((PAIRS_DEV * 16, LANES), jnp.float32)],
        compiler_params=PARAMS,
    )(*near, jnp.asarray(order))


def solution(mesh):
    placed = (P(None, "stn", "src"), P(None, "src"), P("src"), P("src"), P(), P(), P("stn", None))
    return jax.shard_map(
        body, mesh=mesh, in_specs=placed, out_specs=P("stn", "src"), check_vma=False
    )
```

profile of v0, /device:TPU:0, one launch (start us, length us, event | category | flops | bytes accessed | tf_op | source)
XLA Modules:
  0.0 90.0 jit_solution(10468697879076449266)
XLA Ops:
  0.7 2.6 %shard_map.82 = bf16[8,528,128]{2,1,0:T(8,128)(2,1)} custom-call(s32[1]{0:T(128)S(6)} %copy.13.live_ref, f32[2,1024]{1,0:T(2,128)} %lm_hbm.1, f32[1,1024]{1,0:T(1,128)} %bitcast.16, s32[2,17]{1,0:T(2,128)} %bitcast.17, bf16[8,64,1024]{2,1,0:T(8,128)(2,1)} %jones_hbm.1), custom_call_target="tpu_custom_call" | custom-call | tf_op jit(solution)/shard_map/pallas_call | solution.py:249
  3.2 0.0 copy-start.2
  3.2 5.5 %all-to-all-start = ((bf16[8,528,128]{2,1,0:T(8,128)(2,1)}), bf16[8,528,128]{2,1,0:T(8,128)(2,1)S(1)}, u32[]{:S(2)}, u32[]{:S(2)}) async-start(bf16[8,528,128]{2,1,0:T(8,128)(2,1)} %shard_map.82), calls=%async_computation | async-start | bytes 2162688 | tf_op jit(solution)/shard_map/all_to_all | solution.py:265
  8.7 0.1 fusion.7
  8.8 0.0 copy-done.2
  8.8 15.1 %all-to-all-done.refs_3_ = bf16[8,528,128]{2,1,0:T(8,128)(2,1)S(1)} async-done(((bf16[8,528,128]{2,1,0:T(8,128)(2,1)}), bf16[8,528,128]{2,1,0:T(8,128)(2,1)S(1)}, u32[]{:S(2)}, u32[]{:S(2)}) %all-to-all-start) | async-done | bytes 1081376 | tf_op jit(solution)/shard_map/all_to_all | solution.py:265
  23.9 0.0 collective-permute-start
  23.9 0.1 add.189
  24.0 0.1 reshape.406
  24.0 0.6 gather_fusion
  24.7 0.1 pad_add_fusion.refs_1_.int_ref
  24.8 0.1 fusion.2
  24.9 0.0 copy-start.1
  24.9 1.1 %fusion.8 = (bf16[4,528,128]{2,1,0:T(8,128)(2,1)}, bf16[4,528,128]{2,1,0:T(8,128)(2,1)}) fusion(bf16[8,528,128]{2,1,0:T(8,128)(2,1)S(1)} %all-to-all-done.refs_3_), kind=kLoop, calls=%fused_computation.36 | loop fusion | bytes 2162688 | tf_op jit(solution)/shard_map/slice | solution.py:266
  26.0 1.9 %collective-permute-start.2 = (bf16[4,528,128]{2,1,0:T(8,128)(2,1)}, bf16[4,528,128]{2,1,0:T(8,128)(2,1)S(1)}, u32[]{:S(2)}, u32[]{:S(2)}) collective-permute-start(bf16[4,528,128]{2,1,0:T(8,128)(2,1)} %get-tuple-element.57), channel_id=1, source_target_pairs={{0,4},{1,13},{2,6},{3,15},{4,8},{5,1},{6,10},{7,3},{8,12},{9,5},{1... | collective-permute-start | bytes 1622024 | tf_op jit(solution)/shard_map/ppermute | solution.py:241
  27.9 1.9 %collective-permute-start.1 = (bf16[4,528,128]{2,1,0:T(8,128)(2,1)}, bf16[4,528,128]{2,1,0:T(8,128)(2,1)S(1)}, u32[]{:S(2)}, u32[]{:S(2)}) collective-permute-start(bf16[4,528,128]{2,1,0:T(8,128)(2,1)} %get-tuple-element.58), channel_id=1, source_target_pairs={{0,4},{1,13},{2,6},{3,15},{4,8},{5,1},{6,10},{7,3},{8,12},{9,5},{1... | collective-permute-start | bytes 1622024 | tf_op jit(solution)/shard_map/ppermute | solution.py:241
  29.8 0.0 collective-permute-done.refs_4_
  29.9 0.1 add.177
  29.9 0.0 copy-done.1
  29.9 0.3 broadcast_in_dim.46.refs_2_.refs_3_
  30.2 3.7 %shard_map.84.refs_5_ = f32[2560,256]{1,0:T(8,128)S(1)} custom-call(f32[2]{0:T(128)S(1)} %gather_fusion, s32[2]{0:T(128)S(1)} %pad_add_fusion.refs_1_.int_ref, f32[3,512,128]{2,1,0:T(8,128)S(1)} %broadcast_in_dim.46.refs_2_.refs_3_, bf16[8,528,128]{2,1,0:T(8,128)(2,1)S(1)} %all-to-all-done.refs_3_, bf16[8,528,128]{2,1,0:T(8,128)(2,1)S(1)} %collective-permute-done.refs_4_), custom_call_target="tpu_custom_call" | custom-call | tf_op jit(solution)/shard_map/pallas_call | solution.py:288
  33.9 3.7 %shard_map.83.refs_8_ = f32[2560,256]{1,0:T(8,128)S(1)} custom-call(f32[2]{0:T(128)S(1)} %gather_fusion, s32[2]{0:T(128)S(1)} %pad_add_fusion.refs_1_.int_ref, f32[3,512,128]{2,1,0:T(8,128)S(1)} %broadcast_in_dim.46.refs_2_.refs_3_, bf16[8,528,128]{2,1,0:T(8,128)(2,1)S(1)} %all-to-all-done.refs_3_, bf16[8,528,128]{2,1,0:T(8,128)(2,1)S(1)} %collective-permute-done.refs_4_), custom_call_target="tpu_custom_call" | custom-call | tf_op jit(solution)/shard_map/pallas_call | solution.py:288
  37.7 0.0 collective-permute-done.2.refs_4_.refs_5_
  37.7 5.6 %collective-permute-done.1.refs_3_.refs_4_ = bf16[4,528,128]{2,1,0:T(8,128)(2,1)S(1)} collective-permute-done((bf16[4,528,128]{2,1,0:T(8,128)(2,1)}, bf16[4,528,128]{2,1,0:T(8,128)(2,1)S(1)}, u32[]{:S(2)}, u32[]{:S(2)}) %collective-permute-start.1) | collective-permute-done | bytes 540704 | tf_op jit(solution)/shard_map/ppermute | solution.py:241
  43.3 0.0 collective-permute-start.3
  43.3 0.5 collective-permute-start.4
  43.8 0.1 iota_compare_fusion
  43.9 0.2 select_reduce_fusion
  44.1 2.4 %shard_map.85.refs_6_ = f32[2560,256]{1,0:T(8,128)S(1)} custom-call(f32[2]{0:T(128)S(1)} %gather_fusion, s32[2]{0:T(128)S(1)} %pad_add_fusion.refs_1_.int_ref, f32[3,512,128]{2,1,0:T(8,128)S(1)} %broadcast_in_dim.46.refs_2_.refs_3_, bf16[4,528,128]{2,1,0:T(8,128)(2,1)S(1)} %collective-permute-done.1.refs_3_.refs_4_, ...), custom_call_target="tpu_custom_call", output_to_operand_aliasing={{}: (5, {})} | custom-call | tf_op jit(solution)/shard_map/pallas_call | solution.py:288
  46.6 0.0 collective-permute-done.3.refs_4_.refs_6_
  46.6 0.0 collective-permute-done.4.refs_5_.refs_7_
  46.6 3.0 %shard_map.86 = (bf16[68,16,128]{2,1,0:T(8,128)(2,1)S(1)}, bf16[68,16,128]{2,1,0:T(8,128)(2,1)S(1)}, bf16[68,16,128]{2,1,0:T(8,128)(2,1)S(1)}, bf16[68,16,128]{2,1,0:T(8,128)(2,1)S(1)}) custom-call(f32[2]{0:T(128)S(1)} %gather_fusion, s32[2]{0:T(128)S(1)} %pad_add_fusion.refs_1_.int_ref, s32[512]{0:T(512)S(1)} %bitcast.14, ...), custom_call_target="tpu_custom_call" | custom-call | tf_op jit(solution)/shard_map/pallas_call | solution.py:288
  49.6 0.9 %collective-permute-start.8 = (bf16[68,16,128]{2,1,0:T(8,128)(2,1)S(1)}, bf16[68,16,128]{2,1,0:T(8,128)(2,1)S(1)}, u32[]{:S(2)}, u32[]{:S(2)}) collective-permute-start(bf16[68,16,128]{2,1,0:T(8,128)(2,1)S(1)} %get-tuple-element.48), channel_id=1, source_target_pairs={{0,16},{1,17},{2,18},{3,19},{4,20},{5,21},{6,22},{7,23},{8,24},{9,... | collective-permute-start | bytes 835592 | tf_op jit(solution)/shard_map/ppermute | solution.py:241
  50.5 2.1 %collective-permute-start.9 = (bf16[68,16,128]{2,1,0:T(8,128)(2,1)S(1)}, bf16[68,16,128]{2,1,0:T(8,128)(2,1)S(1)}, u32[]{:S(2)}, u32[]{:S(2)}) collective-permute-start(bf16[68,16,128]{2,1,0:T(8,128)(2,1)S(1)} %get-tuple-element.49), channel_id=1, source_target_pairs={{0,32},{1,33},{2,34},{3,35},{4,36},{5,37},{6,38},{7,39},{8,40},{9,... | collective-permute-start | bytes 835592 | tf_op jit(solution)/shard_map/ppermute | solution.py:241
  52.6 1.5 %collective-permute-start.10 = (bf16[68,16,128]{2,1,0:T(8,128)(2,1)S(1)}, bf16[68,16,128]{2,1,0:T(8,128)(2,1)S(1)}, u32[]{:S(2)}, u32[]{:S(2)}) collective-permute-start(bf16[68,16,128]{2,1,0:T(8,128)(2,1)S(1)} %get-tuple-element.50), channel_id=1, source_target_pairs={{0,48},{1,49},{2,50},{3,51},{4,52},{5,53},{6,54},{7,55},{8,56},{9,... | collective-permute-start | bytes 835592 | tf_op jit(solution)/shard_map/ppermute | solution.py:241
  54.1 4.3 %shard_map.87 = (bf16[68,16,128]{2,1,0:T(8,128)(2,1)S(1)}, bf16[68,16,128]{2,1,0:T(8,128)(2,1)S(1)}, bf16[68,16,128]{2,1,0:T(8,128)(2,1)S(1)}, bf16[68,16,128]{2,1,0:T(8,128)(2,1)S(1)}) custom-call(f32[2]{0:T(128)S(1)} %gather_fusion, s32[2]{0:T(128)S(1)} %pad_add_fusion.refs_1_.int_ref, s32[512]{0:T(512)S(1)} %bitcast.15, ...), custom_call_target="tpu_custom_call" | custom-call | tf_op jit(solution)/shard_map/pallas_call | solution.py:288
  58.5 0.6 collective-permute-start.5
  59.1 1.4 %collective-permute-start.6 = (bf16[68,16,128]{2,1,0:T(8,128)(2,1)S(1)}, bf16[68,16,128]{2,1,0:T(8,128)(2,1)S(1)}, u32[]{:S(2)}, u32[]{:S(2)}) collective-permute-start(bf16[68,16,128]{2,1,0:T(8,128)(2,1)S(1)} %get-tuple-element.45), channel_id=1, source_target_pairs={{0,32},{1,33},{2,34},{3,35},{4,36},{5,37},{6,38},{7,39},{8,40},{9,... | collective-permute-start | bytes 835592 | tf_op jit(solution)/shard_map/ppermute | solution.py:241
  60.5 4.5 %collective-permute-done.8.two = bf16[68,16,128]{2,1,0:T(8,128)(2,1)S(1)} collective-permute-done((bf16[68,16,128]{2,1,0:T(8,128)(2,1)S(1)}, bf16[68,16,128]{2,1,0:T(8,128)(2,1)S(1)}, u32[]{:S(2)}, u32[]{:S(2)}) %collective-permute-start.8) | collective-permute-done | bytes 278560 | tf_op jit(solution)/shard_map/ppermute | solution.py:241
  65.0 0.0 copy-start
  65.0 0.0 collective-permute-start.7
  65.0 1.1 %collective-permute-done.9.three = bf16[68,16,128]{2,1,0:T(8,128)(2,1)S(1)} collective-permute-done((bf16[68,16,128]{2,1,0:T(8,128)(2,1)S(1)}, bf16[68,16,128]{2,1,0:T(8,128)(2,1)S(1)}, u32[]{:S(2)}, u32[]{:S(2)}) %collective-permute-start.9) | collective-permute-done | bytes 278560 | tf_op jit(solution)/shard_map/ppermute | solution.py:241
  66.1 1.1 %collective-permute-done.10.four = bf16[68,16,128]{2,1,0:T(8,128)(2,1)S(1)} collective-permute-done((bf16[68,16,128]{2,1,0:T(8,128)(2,1)S(1)}, bf16[68,16,128]{2,1,0:T(8,128)(2,1)S(1)}, u32[]{:S(2)}, u32[]{:S(2)}) %collective-permute-start.10) | collective-permute-done | bytes 278560 | tf_op jit(solution)/shard_map/ppermute | solution.py:241
  67.3 0.1 shard_map.88
  67.4 1.9 %collective-permute-start.11 = (f32[34,16,128]{2,1,0:T(8,128)S(1)}, f32[34,16,128]{2,1,0:T(8,128)S(1)}, u32[]{:S(2)}, u32[]{:S(2)}) collective-permute-start(f32[34,16,128]{2,1,0:T(8,128)S(1)} %get-tuple-element.51), channel_id=1, source_target_pairs={{0,8},{1,9},{2,10},{3,11},{4,12},{5,13},{6,14},{7,15},{8,0},{9,1},... | collective-permute-start | bytes 835592 | tf_op jit(solution)/shard_map/ppermute | solution.py:241
  69.4 1.7 %collective-permute-start.12 = (bf16[34,16,128]{2,1,0:T(8,128)(2,1)S(1)}, bf16[34,16,128]{2,1,0:T(8,128)(2,1)S(1)}, u32[]{:S(2)}, u32[]{:S(2)}) collective-permute-start(bf16[34,16,128]{2,1,0:T(8,128)(2,1)S(1)} %get-tuple-element.52), channel_id=1, source_target_pairs={{0,8},{1,9},{2,10},{3,11},{4,12},{5,13},{6,14},{7,15},{8,0},{9,1},... | collective-permute-start | bytes 417800 | tf_op jit(solution)/shard_map/ppermute | solution.py:241
  71.0 6.4 %collective-permute-done.5.two = bf16[68,16,128]{2,1,0:T(8,128)(2,1)S(1)} collective-permute-done((bf16[68,16,128]{2,1,0:T(8,128)(2,1)S(1)}, bf16[68,16,128]{2,1,0:T(8,128)(2,1)S(1)}, u32[]{:S(2)}, u32[]{:S(2)}) %collective-permute-start.5) | collective-permute-done | bytes 278560 | tf_op jit(solution)/shard_map/ppermute | solution.py:241
  77.4 0.0 collective-permute-done.6.three
  77.4 0.7 collective-permute-done.7.four
  78.1 0.8 collective-permute-done.12.imag_ref
  78.9 0.0 collective-permute-done.11.real_ref
  78.9 0.7 shard_map.89
  79.6 1.5 %collective-permute-start.13 = (f32[272,128]{1,0:T(8,128)S(1)}, f32[272,128]{1,0:T(8,128)S(1)}, u32[]{:S(2)}, u32[]{:S(2)}) collective-permute-start(f32[272,128]{1,0:T(8,128)S(1)} %get-tuple-element.54), channel_id=1, source_target_pairs={{0,64},{1,65},{2,66},{3,67},{4,68},{5,69},{6,70},{7,71},{8,72},{9,... | collective-permute-start | bytes 417800 | tf_op jit(solution)/shard_map/ppermute | solution.py:241
  81.1 2.7 %collective-permute-start.14 = (f32[272,128]{1,0:T(8,128)S(1)}, f32[272,128]{1,0:T(8,128)S(1)}, u32[]{:S(2)}, u32[]{:S(2)}) collective-permute-start(f32[272,128]{1,0:T(8,128)S(1)} %get-tuple-element.55), channel_id=1, source_target_pairs={{0,2},{1,3},{2,0},{3,1},{4,6},{5,7},{6,4},{7,5},{8,10},{9,11},{10,... | collective-permute-start | bytes 417800 | tf_op jit(solution)/shard_map/ppermute | solution.py:241
  83.9 1.2 %collective-permute-start.15 = (f32[272,128]{1,0:T(8,128)S(1)}, f32[272,128]{1,0:T(8,128)S(1)}, u32[]{:S(2)}, u32[]{:S(2)}) collective-permute-start(f32[272,128]{1,0:T(8,128)S(1)} %get-tuple-element.56), channel_id=1, source_target_pairs={{0,66},{1,67},{2,64},{3,65},{4,70},{5,71},{6,68},{7,69},{8,74},{9,... | collective-permute-start | bytes 417800 | tf_op jit(solution)/shard_map/ppermute | solution.py:241
  85.0 2.4 %collective-permute-done.13.refs_1_ = f32[272,128]{1,0:T(8,128)S(1)} collective-permute-done((f32[272,128]{1,0:T(8,128)S(1)}, f32[272,128]{1,0:T(8,128)S(1)}, u32[]{:S(2)}, u32[]{:S(2)}) %collective-permute-start.13) | collective-permute-done | bytes 139296 | tf_op jit(solution)/shard_map/ppermute | solution.py:241
  87.4 1.5 %collective-permute-done.14.refs_2_ = f32[272,128]{1,0:T(8,128)S(1)} collective-permute-done((f32[272,128]{1,0:T(8,128)S(1)}, f32[272,128]{1,0:T(8,128)S(1)}, u32[]{:S(2)}, u32[]{:S(2)}) %collective-permute-start.14) | collective-permute-done | bytes 139296 | tf_op jit(solution)/shard_map/ppermute | solution.py:241
  89.0 0.0 collective-permute-done.15.refs_3_
  89.0 0.0 copy-done
  89.0 1.0 %shard_map.90 = f32[17,2048]{1,0:T(8,128)} custom-call(f32[272,128]{1,0:T(8,128)S(1)} %get-tuple-element.53.refs_0_, f32[272,128]{1,0:T(8,128)S(1)} %collective-permute-done.13.refs_1_, f32[272,128]{1,0:T(8,128)S(1)} %collective-permute-done.14.refs_2_, f32[272,128]{1,0:T(8,128)S(1)} %collective-permute-done.15.refs_3_, f32[128,128]{1,0:T(8,128)S(1)} %copy-done), custom_call_target="tpu_custom_call" | custom-call | tf_op jit(solution)/shard_map/pallas_call | solution.py:327
  (12 shorter events, 0.1 us)
Async XLA Ops:
  3.2 5.6 %copy-start.2 = (f32[4]{0:T(128)S(1)}, f32[4]{0:T(128)}, u32[]{:S(2)}) copy-start(f32[4]{0:T(128)} %param.13) | copy-start | bytes 52
  3.2 20.6 %all-to-all-start = ((bf16[8,528,128]{2,1,0:T(8,128)(2,1)}), bf16[8,528,128]{2,1,0:T(8,128)(2,1)S(1)}, u32[]{:S(2)}, u32[]{:S(2)}) async-start(bf16[8,528,128]{2,1,0:T(8,128)(2,1)} %shard_map.82), calls=%async_computation | async-start | bytes 2162688 | tf_op jit(solution)/shard_map/all_to_all | solution.py:265
  23.9 5.9 %collective-permute-start = (bf16[8,528,128]{2,1,0:T(8,128)(2,1)S(1)}, bf16[8,528,128]{2,1,0:T(8,128)(2,1)S(1)}, u32[]{:S(2)}, u32[]{:S(2)}) collective-permute-start(bf16[8,528,128]{2,1,0:T(8,128)(2,1)S(1)} %all-to-all-done.refs_3_), channel_id=1, source_target_pairs={{0,1},{1,0},{2,3},{3,2},{4,5},{5,4},{6,7},{7,6},{8,9},{9,8},{10,11... | collective-permute-start | bytes 3244040 | tf_op jit(solution)/shard_map/ppermute | solution.py:241
  24.9 5.1 %copy-start.1 = (f32[3,512]{1,0:T(4,128)S(1)}, f32[3,512]{1,0:T(4,128)}, u32[]{:S(2)}) copy-start(f32[3,512]{1,0:T(4,128)} %param.12) | copy-start | bytes 18436
  26.0 11.7 %collective-permute-start.2 = (bf16[4,528,128]{2,1,0:T(8,128)(2,1)}, bf16[4,528,128]{2,1,0:T(8,128)(2,1)S(1)}, u32[]{:S(2)}, u32[]{:S(2)}) collective-permute-start(bf16[4,528,128]{2,1,0:T(8,128)(2,1)} %get-tuple-element.57), channel_id=1, source_target_pairs={{0,4},{1,13},{2,6},{3,15},{4,8},{5,1},{6,10},{7,3},{8,12},{9,5},{1... | collective-permute-start | bytes 1622024 | tf_op jit(solution)/shard_map/ppermute | solution.py:241
  27.9 15.5 %collective-permute-start.1 = (bf16[4,528,128]{2,1,0:T(8,128)(2,1)}, bf16[4,528,128]{2,1,0:T(8,128)(2,1)S(1)}, u32[]{:S(2)}, u32[]{:S(2)}) collective-permute-start(bf16[4,528,128]{2,1,0:T(8,128)(2,1)} %get-tuple-element.58), channel_id=1, source_target_pairs={{0,4},{1,13},{2,6},{3,15},{4,8},{5,1},{6,10},{7,3},{8,12},{9,5},{1... | collective-permute-start | bytes 1622024 | tf_op jit(solution)/shard_map/ppermute | solution.py:241
  43.3 3.2 %collective-permute-start.3 = (bf16[4,528,128]{2,1,0:T(8,128)(2,1)S(1)}, bf16[4,528,128]{2,1,0:T(8,128)(2,1)S(1)}, u32[]{:S(2)}, u32[]{:S(2)}) collective-permute-start(bf16[4,528,128]{2,1,0:T(8,128)(2,1)S(1)} %collective-permute-done.1.refs_3_.refs_4_), channel_id=1, source_target_pairs={{0,1},{1,0},{2,3},{3,2},{4,5},{5,4},{6,7},{7,6},{8,9},{9,8},{10,11... | collective-permute-start | bytes 1622024 | tf_op jit(solution)/shard_map/ppermute | solution.py:241
  43.3 3.2 %collective-permute-start.4 = (bf16[4,528,128]{2,1,0:T(8,128)(2,1)S(1)}, bf16[4,528,128]{2,1,0:T(8,128)(2,1)S(1)}, u32[]{:S(2)}, u32[]{:S(2)}) collective-permute-start(bf16[4,528,128]{2,1,0:T(8,128)(2,1)S(1)} %collective-permute-done.2.refs_4_.refs_5_), channel_id=1, source_target_pairs={{0,1},{1,0},{2,3},{3,2},{4,5},{5,4},{6,7},{7,6},{8,9},{9,8},{10,11... | collective-permute-start | bytes 1622024 | tf_op jit(solution)/shard_map/ppermute | solution.py:241
  49.6 15.4 %collective-permute-start.8 = (bf16[68,16,128]{2,1,0:T(8,128)(2,1)S(1)}, bf16[68,16,128]{2,1,0:T(8,128)(2,1)S(1)}, u32[]{:S(2)}, u32[]{:S(2)}) collective-permute-start(bf16[68,16,128]{2,1,0:T(8,128)(2,1)S(1)} %get-tuple-element.48), channel_id=1, source_target_pairs={{0,16},{1,17},{2,18},{3,19},{4,20},{5,21},{6,22},{7,23},{8,24},{9,... | collective-permute-start | bytes 835592 | tf_op jit(solution)/shard_map/ppermute | solution.py:241
  50.5 15.6 %collective-permute-start.9 = (bf16[68,16,128]{2,1,0:T(8,128)(2,1)S(1)}, bf16[68,16,128]{2,1,0:T(8,128)(2,1)S(1)}, u32[]{:S(2)}, u32[]{:S(2)}) collective-permute-start(bf16[68,16,128]{2,1,0:T(8,128)(2,1)S(1)} %get-tuple-element.49), channel_id=1, source_target_pairs={{0,32},{1,33},{2,34},{3,35},{4,36},{5,37},{6,38},{7,39},{8,40},{9,... | collective-permute-start | bytes 835592 | tf_op jit(solution)/shard_map/ppermute | solution.py:241
  52.6 14.6 %collective-permute-start.10 = (bf16[68,16,128]{2,1,0:T(8,128)(2,1)S(1)}, bf16[68,16,128]{2,1,0:T(8,128)(2,1)S(1)}, u32[]{:S(2)}, u32[]{:S(2)}) collective-permute-start(bf16[68,16,128]{2,1,0:T(8,128)(2,1)S(1)} %get-tuple-element.50), channel_id=1, source_target_pairs={{0,48},{1,49},{2,50},{3,51},{4,52},{5,53},{6,54},{7,55},{8,56},{9,... | collective-permute-start | bytes 835592 | tf_op jit(solution)/shard_map/ppermute | solution.py:241
  58.5 18.9 %collective-permute-start.5 = (bf16[68,16,128]{2,1,0:T(8,128)(2,1)S(1)}, bf16[68,16,128]{2,1,0:T(8,128)(2,1)S(1)}, u32[]{:S(2)}, u32[]{:S(2)}) collective-permute-start(bf16[68,16,128]{2,1,0:T(8,128)(2,1)S(1)} %get-tuple-element.44), channel_id=1, source_target_pairs={{0,16},{1,17},{2,18},{3,19},{4,20},{5,21},{6,22},{7,23},{8,24},{9,... | collective-permute-start | bytes 835592 | tf_op jit(solution)/shard_map/ppermute | solution.py:241
  59.1 18.3 %collective-permute-start.6 = (bf16[68,16,128]{2,1,0:T(8,128)(2,1)S(1)}, bf16[68,16,128]{2,1,0:T(8,128)(2,1)S(1)}, u32[]{:S(2)}, u32[]{:S(2)}) collective-permute-start(bf16[68,16,128]{2,1,0:T(8,128)(2,1)S(1)} %get-tuple-element.45), channel_id=1, source_target_pairs={{0,32},{1,33},{2,34},{3,35},{4,36},{5,37},{6,38},{7,39},{8,40},{9,... | collective-permute-start | bytes 835592 | tf_op jit(solution)/shard_map/ppermute | solution.py:241
  65.0 24.0 %copy-start = (f32[128,128]{1,0:T(8,128)S(1)}, f32[128,128]{1,0:T(8,128)}, u32[]{:S(2)}) copy-start(f32[128,128]{1,0:T(8,128)} %constant.111.clone.refs_4_) | copy-start | bytes 196612
  65.0 13.1 %collective-permute-start.7 = (bf16[68,16,128]{2,1,0:T(8,128)(2,1)S(1)}, bf16[68,16,128]{2,1,0:T(8,128)(2,1)S(1)}, u32[]{:S(2)}, u32[]{:S(2)}) collective-permute-start(bf16[68,16,128]{2,1,0:T(8,128)(2,1)S(1)} %get-tuple-element.46), channel_id=1, source_target_pairs={{0,48},{1,49},{2,50},{3,51},{4,52},{5,53},{6,54},{7,55},{8,56},{9,... | collective-permute-start | bytes 835592 | tf_op jit(solution)/shard_map/ppermute | solution.py:241
  67.4 11.5 %collective-permute-start.11 = (f32[34,16,128]{2,1,0:T(8,128)S(1)}, f32[34,16,128]{2,1,0:T(8,128)S(1)}, u32[]{:S(2)}, u32[]{:S(2)}) collective-permute-start(f32[34,16,128]{2,1,0:T(8,128)S(1)} %get-tuple-element.51), channel_id=1, source_target_pairs={{0,8},{1,9},{2,10},{3,11},{4,12},{5,13},{6,14},{7,15},{8,0},{9,1},... | collective-permute-start | bytes 835592 | tf_op jit(solution)/shard_map/ppermute | solution.py:241
  69.4 9.5 %collective-permute-start.12 = (bf16[34,16,128]{2,1,0:T(8,128)(2,1)S(1)}, bf16[34,16,128]{2,1,0:T(8,128)(2,1)S(1)}, u32[]{:S(2)}, u32[]{:S(2)}) collective-permute-start(bf16[34,16,128]{2,1,0:T(8,128)(2,1)S(1)} %get-tuple-element.52), channel_id=1, source_target_pairs={{0,8},{1,9},{2,10},{3,11},{4,12},{5,13},{6,14},{7,15},{8,0},{9,1},... | collective-permute-start | bytes 417800 | tf_op jit(solution)/shard_map/ppermute | solution.py:241
  79.6 7.8 %collective-permute-start.13 = (f32[272,128]{1,0:T(8,128)S(1)}, f32[272,128]{1,0:T(8,128)S(1)}, u32[]{:S(2)}, u32[]{:S(2)}) collective-permute-start(f32[272,128]{1,0:T(8,128)S(1)} %get-tuple-element.54), channel_id=1, source_target_pairs={{0,64},{1,65},{2,66},{3,67},{4,68},{5,69},{6,70},{7,71},{8,72},{9,... | collective-permute-start | bytes 417800 | tf_op jit(solution)/shard_map/ppermute | solution.py:241
  81.1 7.8 %collective-permute-start.14 = (f32[272,128]{1,0:T(8,128)S(1)}, f32[272,128]{1,0:T(8,128)S(1)}, u32[]{:S(2)}, u32[]{:S(2)}) collective-permute-start(f32[272,128]{1,0:T(8,128)S(1)} %get-tuple-element.55), channel_id=1, source_target_pairs={{0,2},{1,3},{2,0},{3,1},{4,6},{5,7},{6,4},{7,5},{8,10},{9,11},{10,... | collective-permute-start | bytes 417800 | tf_op jit(solution)/shard_map/ppermute | solution.py:241
  83.9 5.1 %collective-permute-start.15 = (f32[272,128]{1,0:T(8,128)S(1)}, f32[272,128]{1,0:T(8,128)S(1)}, u32[]{:S(2)}, u32[]{:S(2)}) collective-permute-start(f32[272,128]{1,0:T(8,128)S(1)} %get-tuple-element.56), channel_id=1, source_target_pairs={{0,66},{1,67},{2,64},{3,65},{4,70},{5,71},{6,68},{7,69},{8,74},{9,... | collective-permute-start | bytes 417800 | tf_op jit(solution)/shard_map/ppermute | solution.py:241
where the time goes:
time: 91.5 us; the launch traced here: 90 us
  waiting for transfers between devices  39.3 us (43%)
  starting transfers between devices  25.4 us (28%)
  Pallas kernels  21.6 us (24%)
  local copies, waits for them, and re-layouts  2.26 us (2%)
    ppermute x16, waiting for transfers between devices, move(): return lax.ppermute(x, ('stn', 'src'), perm)  24.2 us
    ppermute x16, starting transfers between devices, move(): return lax.ppermute(x, ('stn', 'src'), perm)  19.9 us
    pallas_call x5, Pallas kernels, slab(): pl.pallas_call(functools.partial(slab_kernel, chan, packs, chained, [len(...  17.2 us
    all_to_all x1, waiting for transfers between devices, body(): own = lax.all_to_all(message, 'stn', 0, 0, tiled=True)  15.1 us
    all_to_all x1, starting transfers between devices, body(): own = lax.all_to_all(message, 'stn', 0, 0, tiled=True)  5.49 us
    pallas_call x1, Pallas kernels, body(): pl.pallas_call(prep_kernel, out_shape=jax.ShapeDtypeStruct((STN, ROWS, LA...  2.55 us
  transfers between devices with their start and end apart: 17, of which 10 were waited for; matrix products, arithmetic and copies ran while one was open for 3% of the time, Pallas kernels for 16%

commit v1 on v0

--- a/solution.py
+++ b/solution.py
@@ -265,6 +265,7 @@
     own = lax.all_to_all(message, "stn", 0, 0, tiled=True)
     got = [move(own[:4], apart=1), move(own[4:], apart=1)]
     other = move(own, dcore=1)
+    other, chan_scale, station_uvw = lax.optimization_barrier((other, chan_scale, station_uvw))
 
     listed = other[:, JROWS + 12 : JROWS + 14, :PAIRS_DEV].astype(jnp.int32)
     holder = jnp.repeat(jnp.arange(STN, dtype=jnp.int32), PAIRS_DEV)

time: 91.5 us -> 91.1 us (level)
  no operation moved by 1% of the time
where the time goes in v1:
time: 91.1 us; the launch traced here: 89.5 us
  waiting for transfers between devices  38.6 us (42%)
  starting transfers between devices  25.6 us (28%)
  Pallas kernels  21.7 us (24%)
  local copies, waits for them, and re-layouts  2.25 us (2%)
    ppermute x16, waiting for transfers between devices, move(): return lax.ppermute(x, ('stn', 'src'), perm)  23.6 us
    ppermute x16, starting transfers between devices, move(): return lax.ppermute(x, ('stn', 'src'), perm)  20.1 us
    pallas_call x5, Pallas kernels, slab(): pl.pallas_call(functools.partial(slab_kernel, chan, packs, chained, [len(...  17.2 us
    all_to_all x1, waiting for transfers between devices, body(): own = lax.all_to_all(message, 'stn', 0, 0, tiled=True)  15.1 us
    all_to_all x1, starting transfers between devices, body(): own = lax.all_to_all(message, 'stn', 0, 0, tiled=True)  5.49 us
    pallas_call x1, Pallas kernels, body(): pl.pallas_call(prep_kernel, out_shape=jax.ShapeDtypeStruct((STN, ROWS, LA...  2.55 us
  transfers between devices with their start and end apart: 17, of which 10 were waited for; matrix products, arithmetic and copies ran while one was open for 3% of the time, Pallas kernels for 16%

profile of v1, /device:TPU:0, one launch (start us, length us, event | category | flops | bytes accessed | tf_op | source)
XLA Modules:
  0.0 89.5 jit_solution(10447016169872951754)
XLA Ops:
  0.7 2.6 %shard_map.82 = bf16[8,528,128]{2,1,0:T(8,128)(2,1)} custom-call(s32[1]{0:T(128)S(6)} %copy.13.live_ref, f32[2,1024]{1,0:T(2,128)} %lm_hbm.1, f32[1,1024]{1,0:T(1,128)} %bitcast.16, s32[2,17]{1,0:T(2,128)} %bitcast.17, bf16[8,64,1024]{2,1,0:T(8,128)(2,1)} %jones_hbm.1), custom_call_target="tpu_custom_call" | custom-call | tf_op jit(solution)/shard_map/pallas_call | solution.py:249
  3.2 5.5 %all-to-all-start = ((bf16[8,528,128]{2,1,0:T(8,128)(2,1)}), bf16[8,528,128]{2,1,0:T(8,128)(2,1)S(1)}, u32[]{:S(2)}, u32[]{:S(2)}) async-start(bf16[8,528,128]{2,1,0:T(8,128)(2,1)} %shard_map.82), calls=%async_computation | async-start | bytes 2162688 | tf_op jit(solution)/shard_map/all_to_all | solution.py:265
  8.7 0.1 fusion.7
  8.8 15.1 %all-to-all-done.refs_3_ = bf16[8,528,128]{2,1,0:T(8,128)(2,1)S(1)} async-done(((bf16[8,528,128]{2,1,0:T(8,128)(2,1)}), bf16[8,528,128]{2,1,0:T(8,128)(2,1)S(1)}, u32[]{:S(2)}, u32[]{:S(2)}) %all-to-all-start) | async-done | bytes 1081376 | tf_op jit(solution)/shard_map/all_to_all | solution.py:265
  23.9 0.0 collective-permute-start
  23.9 0.1 pad_add_fusion.refs_1_.int_ref
  23.9 0.1 add.189
  24.0 0.1 reshape.406
  24.1 0.1 fusion.2
  24.2 0.0 copy-start.2
  24.2 0.0 copy-start.1
  24.3 1.1 %fusion.8 = (bf16[4,528,128]{2,1,0:T(8,128)(2,1)}, bf16[4,528,128]{2,1,0:T(8,128)(2,1)}) fusion(bf16[8,528,128]{2,1,0:T(8,128)(2,1)S(1)} %all-to-all-done.refs_3_), kind=kLoop, calls=%fused_computation.36 | loop fusion | bytes 2162688 | tf_op jit(solution)/shard_map/slice | solution.py:266
  25.3 1.9 %collective-permute-start.2 = (bf16[4,528,128]{2,1,0:T(8,128)(2,1)}, bf16[4,528,128]{2,1,0:T(8,128)(2,1)S(1)}, u32[]{:S(2)}, u32[]{:S(2)}) collective-permute-start(bf16[4,528,128]{2,1,0:T(8,128)(2,1)} %get-tuple-element.63), channel_id=1, source_target_pairs={{0,4},{1,13},{2,6},{3,15},{4,8},{5,1},{6,10},{7,3},{8,12},{9,5},{1... | collective-permute-start | bytes 1622024 | tf_op jit(solution)/shard_map/ppermute | solution.py:241
  27.3 1.9 %collective-permute-start.1 = (bf16[4,528,128]{2,1,0:T(8,128)(2,1)}, bf16[4,528,128]{2,1,0:T(8,128)(2,1)S(1)}, u32[]{:S(2)}, u32[]{:S(2)}) collective-permute-start(bf16[4,528,128]{2,1,0:T(8,128)(2,1)} %get-tuple-element.64), channel_id=1, source_target_pairs={{0,4},{1,13},{2,6},{3,15},{4,8},{5,1},{6,10},{7,3},{8,12},{9,5},{1... | collective-permute-start | bytes 1622024 | tf_op jit(solution)/shard_map/ppermute | solution.py:241
  29.2 0.0 collective-permute-done.refs_4_
  29.2 0.1 add.177
  29.3 0.0 copy-done.2
  29.3 0.6 gather_fusion
  30.0 0.0 copy-done.1
  30.0 0.3 broadcast_in_dim.46.refs_2_.refs_3_
  30.2 3.7 %shard_map.84.refs_5_ = f32[2560,256]{1,0:T(8,128)S(1)} custom-call(f32[2]{0:T(128)S(1)} %gather_fusion, s32[2]{0:T(128)S(1)} %pad_add_fusion.refs_1_.int_ref, f32[3,512,128]{2,1,0:T(8,128)S(1)} %broadcast_in_dim.46.refs_2_.refs_3_, bf16[8,528,128]{2,1,0:T(8,128)(2,1)S(1)} %all-to-all-done.refs_3_, bf16[8,528,128]{2,1,0:T(8,128)(2,1)S(1)} %collective-permute-done.refs_4_), custom_call_target="tpu_custom_call" | custom-call | tf_op jit(solution)/shard_map/pallas_call | solution.py:289
  34.0 3.7 %shard_map.83.refs_8_ = f32[2560,256]{1,0:T(8,128)S(1)} custom-call(f32[2]{0:T(128)S(1)} %gather_fusion, s32[2]{0:T(128)S(1)} %pad_add_fusion.refs_1_.int_ref, f32[3,512,128]{2,1,0:T(8,128)S(1)} %broadcast_in_dim.46.refs_2_.refs_3_, bf16[8,528,128]{2,1,0:T(8,128)(2,1)S(1)} %all-to-all-done.refs_3_, bf16[8,528,128]{2,1,0:T(8,128)(2,1)S(1)} %collective-permute-done.refs_4_), custom_call_target="tpu_custom_call" | custom-call | tf_op jit(solution)/shard_map/pallas_call | solution.py:289
  37.7 0.0 collective-permute-done.2.refs_4_.refs_5_
  37.7 5.0 %collective-permute-done.1.refs_3_.refs_4_ = bf16[4,528,128]{2,1,0:T(8,128)(2,1)S(1)} collective-permute-done((bf16[4,528,128]{2,1,0:T(8,128)(2,1)}, bf16[4,528,128]{2,1,0:T(8,128)(2,1)S(1)}, u32[]{:S(2)}, u32[]{:S(2)}) %collective-permute-start.1) | collective-permute-done | bytes 540704 | tf_op jit(solution)/shard_map/ppermute | solution.py:241
  42.7 0.0 collective-permute-start.3
  42.7 0.5 collective-permute-start.4
  43.2 0.1 iota_compare_fusion
  43.3 0.2 select_reduce_fusion
  43.5 2.4 %shard_map.85.refs_6_ = f32[2560,256]{1,0:T(8,128)S(1)} custom-call(f32[2]{0:T(128)S(1)} %gather_fusion, s32[2]{0:T(128)S(1)} %pad_add_fusion.refs_1_.int_ref, f32[3,512,128]{2,1,0:T(8,128)S(1)} %broadcast_in_dim.46.refs_2_.refs_3_, bf16[4,528,128]{2,1,0:T(8,128)(2,1)S(1)} %collective-permute-done.1.refs_3_.refs_4_, ...), custom_call_target="tpu_custom_call", output_to_operand_aliasing={{}: (5, {})} | custom-call | tf_op jit(solution)/shard_map/pallas_call | solution.py:289
  46.0 0.0 collective-permute-done.3.refs_4_.refs_6_
  46.0 0.0 collective-permute-done.4.refs_5_.refs_7_
  46.0 3.0 %shard_map.86 = (bf16[68,16,128]{2,1,0:T(8,128)(2,1)S(1)}, bf16[68,16,128]{2,1,0:T(8,128)(2,1)S(1)}, bf16[68,16,128]{2,1,0:T(8,128)(2,1)S(1)}, bf16[68,16,128]{2,1,0:T(8,128)(2,1)S(1)}) custom-call(f32[2]{0:T(128)S(1)} %gather_fusion, s32[2]{0:T(128)S(1)} %pad_add_fusion.refs_1_.int_ref, s32[512]{0:T(512)S(1)} %bitcast.14, ...), custom_call_target="tpu_custom_call" | custom-call | tf_op jit(solution)/shard_map/pallas_call | solution.py:289
  49.0 1.1 %collective-permute-start.8 = (bf16[68,16,128]{2,1,0:T(8,128)(2,1)S(1)}, bf16[68,16,128]{2,1,0:T(8,128)(2,1)S(1)}, u32[]{:S(2)}, u32[]{:S(2)}) collective-permute-start(bf16[68,16,128]{2,1,0:T(8,128)(2,1)S(1)} %get-tuple-element.54), channel_id=1, source_target_pairs={{0,16},{1,17},{2,18},{3,19},{4,20},{5,21},{6,22},{7,23},{8,24},{9,... | collective-permute-start | bytes 835592 | tf_op jit(solution)/shard_map/ppermute | solution.py:241
  50.1 2.1 %collective-permute-start.9 = (bf16[68,16,128]{2,1,0:T(8,128)(2,1)S(1)}, bf16[68,16,128]{2,1,0:T(8,128)(2,1)S(1)}, u32[]{:S(2)}, u32[]{:S(2)}) collective-permute-start(bf16[68,16,128]{2,1,0:T(8,128)(2,1)S(1)} %get-tuple-element.55), channel_id=1, source_target_pairs={{0,32},{1,33},{2,34},{3,35},{4,36},{5,37},{6,38},{7,39},{8,40},{9,... | collective-permute-start | bytes 835592 | tf_op jit(solution)/shard_map/ppermute | solution.py:241
  52.2 1.5 %collective-permute-start.10 = (bf16[68,16,128]{2,1,0:T(8,128)(2,1)S(1)}, bf16[68,16,128]{2,1,0:T(8,128)(2,1)S(1)}, u32[]{:S(2)}, u32[]{:S(2)}) collective-permute-start(bf16[68,16,128]{2,1,0:T(8,128)(2,1)S(1)} %get-tuple-element.56), channel_id=1, source_target_pairs={{0,48},{1,49},{2,50},{3,51},{4,52},{5,53},{6,54},{7,55},{8,56},{9,... | collective-permute-start | bytes 835592 | tf_op jit(solution)/shard_map/ppermute | solution.py:241
  53.7 4.3 %shard_map.87 = (bf16[68,16,128]{2,1,0:T(8,128)(2,1)S(1)}, bf16[68,16,128]{2,1,0:T(8,128)(2,1)S(1)}, bf16[68,16,128]{2,1,0:T(8,128)(2,1)S(1)}, bf16[68,16,128]{2,1,0:T(8,128)(2,1)S(1)}) custom-call(f32[2]{0:T(128)S(1)} %gather_fusion, s32[2]{0:T(128)S(1)} %pad_add_fusion.refs_1_.int_ref, s32[512]{0:T(512)S(1)} %bitcast.15, ...), custom_call_target="tpu_custom_call" | custom-call | tf_op jit(solution)/shard_map/pallas_call | solution.py:289
  58.1 0.6 collective-permute-start.5
  58.6 1.4 %collective-permute-start.6 = (bf16[68,16,128]{2,1,0:T(8,128)(2,1)S(1)}, bf16[68,16,128]{2,1,0:T(8,128)(2,1)S(1)}, u32[]{:S(2)}, u32[]{:S(2)}) collective-permute-start(bf16[68,16,128]{2,1,0:T(8,128)(2,1)S(1)} %get-tuple-element.51), channel_id=1, source_target_pairs={{0,32},{1,33},{2,34},{3,35},{4,36},{5,37},{6,38},{7,39},{8,40},{9,... | collective-permute-start | bytes 835592 | tf_op jit(solution)/shard_map/ppermute | solution.py:241
  60.1 4.5 %collective-permute-done.8.two = bf16[68,16,128]{2,1,0:T(8,128)(2,1)S(1)} collective-permute-done((bf16[68,16,128]{2,1,0:T(8,128)(2,1)S(1)}, bf16[68,16,128]{2,1,0:T(8,128)(2,1)S(1)}, u32[]{:S(2)}, u32[]{:S(2)}) %collective-permute-start.8) | collective-permute-done | bytes 278560 | tf_op jit(solution)/shard_map/ppermute | solution.py:241
  64.5 0.0 copy-start
  64.5 0.0 collective-permute-start.7
  64.5 1.2 %collective-permute-done.9.three = bf16[68,16,128]{2,1,0:T(8,128)(2,1)S(1)} collective-permute-done((bf16[68,16,128]{2,1,0:T(8,128)(2,1)S(1)}, bf16[68,16,128]{2,1,0:T(8,128)(2,1)S(1)}, u32[]{:S(2)}, u32[]{:S(2)}) %collective-permute-start.9) | collective-permute-done | bytes 278560 | tf_op jit(solution)/shard_map/ppermute | solution.py:241
  65.7 1.1 %collective-permute-done.10.four = bf16[68,16,128]{2,1,0:T(8,128)(2,1)S(1)} collective-permute-done((bf16[68,16,128]{2,1,0:T(8,128)(2,1)S(1)}, bf16[68,16,128]{2,1,0:T(8,128)(2,1)S(1)}, u32[]{:S(2)}, u32[]{:S(2)}) %collective-permute-start.10) | collective-permute-done | bytes 278560 | tf_op jit(solution)/shard_map/ppermute | solution.py:241
  66.8 0.1 shard_map.88
  67.0 1.9 %collective-permute-start.11 = (f32[34,16,128]{2,1,0:T(8,128)S(1)}, f32[34,16,128]{2,1,0:T(8,128)S(1)}, u32[]{:S(2)}, u32[]{:S(2)}) collective-permute-start(f32[34,16,128]{2,1,0:T(8,128)S(1)} %get-tuple-element.57), channel_id=1, source_target_pairs={{0,8},{1,9},{2,10},{3,11},{4,12},{5,13},{6,14},{7,15},{8,0},{9,1},... | collective-permute-start | bytes 835592 | tf_op jit(solution)/shard_map/ppermute | solution.py:241
  68.9 1.7 %collective-permute-start.12 = (bf16[34,16,128]{2,1,0:T(8,128)(2,1)S(1)}, bf16[34,16,128]{2,1,0:T(8,128)(2,1)S(1)}, u32[]{:S(2)}, u32[]{:S(2)}) collective-permute-start(bf16[34,16,128]{2,1,0:T(8,128)(2,1)S(1)} %get-tuple-element.58), channel_id=1, source_target_pairs={{0,8},{1,9},{2,10},{3,11},{4,12},{5,13},{6,14},{7,15},{8,0},{9,1},... | collective-permute-start | bytes 417800 | tf_op jit(solution)/shard_map/ppermute | solution.py:241
  70.6 6.4 %collective-permute-done.5.two = bf16[68,16,128]{2,1,0:T(8,128)(2,1)S(1)} collective-permute-done((bf16[68,16,128]{2,1,0:T(8,128)(2,1)S(1)}, bf16[68,16,128]{2,1,0:T(8,128)(2,1)S(1)}, u32[]{:S(2)}, u32[]{:S(2)}) %collective-permute-start.5) | collective-permute-done | bytes 278560 | tf_op jit(solution)/shard_map/ppermute | solution.py:241
  77.0 0.0 collective-permute-done.6.three
  77.0 0.7 collective-permute-done.7.four
  77.6 0.8 collective-permute-done.12.imag_ref
  78.4 0.0 collective-permute-done.11.real_ref
  78.4 0.7 shard_map.89
  79.2 1.5 %collective-permute-start.13 = (f32[272,128]{1,0:T(8,128)S(1)}, f32[272,128]{1,0:T(8,128)S(1)}, u32[]{:S(2)}, u32[]{:S(2)}) collective-permute-start(f32[272,128]{1,0:T(8,128)S(1)} %get-tuple-element.60), channel_id=1, source_target_pairs={{0,64},{1,65},{2,66},{3,67},{4,68},{5,69},{6,70},{7,71},{8,72},{9,... | collective-permute-start | bytes 417800 | tf_op jit(solution)/shard_map/ppermute | solution.py:241
  80.7 2.7 %collective-permute-start.14 = (f32[272,128]{1,0:T(8,128)S(1)}, f32[272,128]{1,0:T(8,128)S(1)}, u32[]{:S(2)}, u32[]{:S(2)}) collective-permute-start(f32[272,128]{1,0:T(8,128)S(1)} %get-tuple-element.61), channel_id=1, source_target_pairs={{0,2},{1,3},{2,0},{3,1},{4,6},{5,7},{6,4},{7,5},{8,10},{9,11},{10,... | collective-permute-start | bytes 417800 | tf_op jit(solution)/shard_map/ppermute | solution.py:241
  83.4 1.2 %collective-permute-start.15 = (f32[272,128]{1,0:T(8,128)S(1)}, f32[272,128]{1,0:T(8,128)S(1)}, u32[]{:S(2)}, u32[]{:S(2)}) collective-permute-start(f32[272,128]{1,0:T(8,128)S(1)} %get-tuple-element.62), channel_id=1, source_target_pairs={{0,66},{1,67},{2,64},{3,65},{4,70},{5,71},{6,68},{7,69},{8,74},{9,... | collective-permute-start | bytes 417800 | tf_op jit(solution)/shard_map/ppermute | solution.py:241
  84.6 2.4 %collective-permute-done.13.refs_1_ = f32[272,128]{1,0:T(8,128)S(1)} collective-permute-done((f32[272,128]{1,0:T(8,128)S(1)}, f32[272,128]{1,0:T(8,128)S(1)}, u32[]{:S(2)}, u32[]{:S(2)}) %collective-permute-start.13) | collective-permute-done | bytes 139296 | tf_op jit(solution)/shard_map/ppermute | solution.py:241
  87.0 1.6 %collective-permute-done.14.refs_2_ = f32[272,128]{1,0:T(8,128)S(1)} collective-permute-done((f32[272,128]{1,0:T(8,128)S(1)}, f32[272,128]{1,0:T(8,128)S(1)}, u32[]{:S(2)}, u32[]{:S(2)}) %collective-permute-start.14) | collective-permute-done | bytes 139296 | tf_op jit(solution)/shard_map/ppermute | solution.py:241
  88.6 0.0 collective-permute-done.15.refs_3_
  88.6 0.0 copy-done
  88.6 1.0 %shard_map.90 = f32[17,2048]{1,0:T(8,128)} custom-call(f32[272,128]{1,0:T(8,128)S(1)} %get-tuple-element.59.refs_0_, f32[272,128]{1,0:T(8,128)S(1)} %collective-permute-done.13.refs_1_, f32[272,128]{1,0:T(8,128)S(1)} %collective-permute-done.14.refs_2_, f32[272,128]{1,0:T(8,128)S(1)} %collective-permute-done.15.refs_3_, f32[128,128]{1,0:T(8,128)S(1)} %copy-done), custom_call_target="tpu_custom_call" | custom-call | tf_op jit(solution)/shard_map/pallas_call | solution.py:328
  (12 shorter events, 0.1 us)
Async XLA Ops:
  3.2 20.6 %all-to-all-start = ((bf16[8,528,128]{2,1,0:T(8,128)(2,1)}), bf16[8,528,128]{2,1,0:T(8,128)(2,1)S(1)}, u32[]{:S(2)}, u32[]{:S(2)}) async-start(bf16[8,528,128]{2,1,0:T(8,128)(2,1)} %shard_map.82), calls=%async_computation | async-start | bytes 2162688 | tf_op jit(solution)/shard_map/all_to_all | solution.py:265
  23.9 5.3 %collective-permute-start = (bf16[8,528,128]{2,1,0:T(8,128)(2,1)S(1)}, bf16[8,528,128]{2,1,0:T(8,128)(2,1)S(1)}, u32[]{:S(2)}, u32[]{:S(2)}) collective-permute-start(bf16[8,528,128]{2,1,0:T(8,128)(2,1)S(1)} %all-to-all-done.refs_3_), channel_id=1, source_target_pairs={{0,1},{1,0},{2,3},{3,2},{4,5},{5,4},{6,7},{7,6},{8,9},{9,8},{10,11... | collective-permute-start | bytes 3244040 | tf_op jit(solution)/shard_map/ppermute | solution.py:241
  24.2 5.1 %copy-start.2 = (f32[4]{0:T(128)S(1)}, f32[4]{0:T(128)}, u32[]{:S(2)}) copy-start(f32[4]{0:T(128)} %param.13) | copy-start | bytes 52
  24.2 5.7 %copy-start.1 = (f32[3,512]{1,0:T(4,128)S(1)}, f32[3,512]{1,0:T(4,128)}, u32[]{:S(2)}) copy-start(f32[3,512]{1,0:T(4,128)} %param.12) | copy-start | bytes 18436
  25.3 12.4 %collective-permute-start.2 = (bf16[4,528,128]{2,1,0:T(8,128)(2,1)}, bf16[4,528,128]{2,1,0:T(8,128)(2,1)S(1)}, u32[]{:S(2)}, u32[]{:S(2)}) collective-permute-start(bf16[4,528,128]{2,1,0:T(8,128)(2,1)} %get-tuple-element.63), channel_id=1, source_target_pairs={{0,4},{1,13},{2,6},{3,15},{4,8},{5,1},{6,10},{7,3},{8,12},{9,5},{1... | collective-permute-start | bytes 1622024 | tf_op jit(solution)/shard_map/ppermute | solution.py:241
  27.3 15.5 %collective-permute-start.1 = (bf16[4,528,128]{2,1,0:T(8,128)(2,1)}, bf16[4,528,128]{2,1,0:T(8,128)(2,1)S(1)}, u32[]{:S(2)}, u32[]{:S(2)}) collective-permute-start(bf16[4,528,128]{2,1,0:T(8,128)(2,1)} %get-tuple-element.64), channel_id=1, source_target_pairs={{0,4},{1,13},{2,6},{3,15},{4,8},{5,1},{6,10},{7,3},{8,12},{9,5},{1... | collective-permute-start | bytes 1622024 | tf_op jit(solution)/shard_map/ppermute | solution.py:241
  42.7 3.2 %collective-permute-start.3 = (bf16[4,528,128]{2,1,0:T(8,128)(2,1)S(1)}, bf16[4,528,128]{2,1,0:T(8,128)(2,1)S(1)}, u32[]{:S(2)}, u32[]{:S(2)}) collective-permute-start(bf16[4,528,128]{2,1,0:T(8,128)(2,1)S(1)} %collective-permute-done.1.refs_3_.refs_4_), channel_id=1, source_target_pairs={{0,1},{1,0},{2,3},{3,2},{4,5},{5,4},{6,7},{7,6},{8,9},{9,8},{10,11... | collective-permute-start | bytes 1622024 | tf_op jit(solution)/shard_map/ppermute | solution.py:241
  42.7 3.3 %collective-permute-start.4 = (bf16[4,528,128]{2,1,0:T(8,128)(2,1)S(1)}, bf16[4,528,128]{2,1,0:T(8,128)(2,1)S(1)}, u32[]{:S(2)}, u32[]{:S(2)}) collective-permute-start(bf16[4,528,128]{2,1,0:T(8,128)(2,1)S(1)} %collective-permute-done.2.refs_4_.refs_5_), channel_id=1, source_target_pairs={{0,1},{1,0},{2,3},{3,2},{4,5},{5,4},{6,7},{7,6},{8,9},{9,8},{10,11... | collective-permute-start | bytes 1622024 | tf_op jit(solution)/shard_map/ppermute | solution.py:241
  49.0 15.6 %collective-permute-start.8 = (bf16[68,16,128]{2,1,0:T(8,128)(2,1)S(1)}, bf16[68,16,128]{2,1,0:T(8,128)(2,1)S(1)}, u32[]{:S(2)}, u32[]{:S(2)}) collective-permute-start(bf16[68,16,128]{2,1,0:T(8,128)(2,1)S(1)} %get-tuple-element.54), channel_id=1, source_target_pairs={{0,16},{1,17},{2,18},{3,19},{4,20},{5,21},{6,22},{7,23},{8,24},{9,... | collective-permute-start | bytes 835592 | tf_op jit(solution)/shard_map/ppermute | solution.py:241
  50.1 15.6 %collective-permute-start.9 = (bf16[68,16,128]{2,1,0:T(8,128)(2,1)S(1)}, bf16[68,16,128]{2,1,0:T(8,128)(2,1)S(1)}, u32[]{:S(2)}, u32[]{:S(2)}) collective-permute-start(bf16[68,16,128]{2,1,0:T(8,128)(2,1)S(1)} %get-tuple-element.55), channel_id=1, source_target_pairs={{0,32},{1,33},{2,34},{3,35},{4,36},{5,37},{6,38},{7,39},{8,40},{9,... | collective-permute-start | bytes 835592 | tf_op jit(solution)/shard_map/ppermute | solution.py:241
  52.2 14.7 %collective-permute-start.10 = (bf16[68,16,128]{2,1,0:T(8,128)(2,1)S(1)}, bf16[68,16,128]{2,1,0:T(8,128)(2,1)S(1)}, u32[]{:S(2)}, u32[]{:S(2)}) collective-permute-start(bf16[68,16,128]{2,1,0:T(8,128)(2,1)S(1)} %get-tuple-element.56), channel_id=1, source_target_pairs={{0,48},{1,49},{2,50},{3,51},{4,52},{5,53},{6,54},{7,55},{8,56},{9,... | collective-permute-start | bytes 835592 | tf_op jit(solution)/shard_map/ppermute | solution.py:241
  58.1 18.9 %collective-permute-start.5 = (bf16[68,16,128]{2,1,0:T(8,128)(2,1)S(1)}, bf16[68,16,128]{2,1,0:T(8,128)(2,1)S(1)}, u32[]{:S(2)}, u32[]{:S(2)}) collective-permute-start(bf16[68,16,128]{2,1,0:T(8,128)(2,1)S(1)} %get-tuple-element.50), channel_id=1, source_target_pairs={{0,16},{1,17},{2,18},{3,19},{4,20},{5,21},{6,22},{7,23},{8,24},{9,... | collective-permute-start | bytes 835592 | tf_op jit(solution)/shard_map/ppermute | solution.py:241
  58.6 18.3 %collective-permute-start.6 = (bf16[68,16,128]{2,1,0:T(8,128)(2,1)S(1)}, bf16[68,16,128]{2,1,0:T(8,128)(2,1)S(1)}, u32[]{:S(2)}, u32[]{:S(2)}) collective-permute-start(bf16[68,16,128]{2,1,0:T(8,128)(2,1)S(1)} %get-tuple-element.51), channel_id=1, source_target_pairs={{0,32},{1,33},{2,34},{3,35},{4,36},{5,37},{6,38},{7,39},{8,40},{9,... | collective-permute-start | bytes 835592 | tf_op jit(solution)/shard_map/ppermute | solution.py:241
  64.5 24.0 %copy-start = (f32[128,128]{1,0:T(8,128)S(1)}, f32[128,128]{1,0:T(8,128)}, u32[]{:S(2)}) copy-start(f32[128,128]{1,0:T(8,128)} %constant.111.clone.refs_4_) | copy-start | bytes 196612
  64.5 13.1 %collective-permute-start.7 = (bf16[68,16,128]{2,1,0:T(8,128)(2,1)S(1)}, bf16[68,16,128]{2,1,0:T(8,128)(2,1)S(1)}, u32[]{:S(2)}, u32[]{:S(2)}) collective-permute-start(bf16[68,16,128]{2,1,0:T(8,128)(2,1)S(1)} %get-tuple-element.52), channel_id=1, source_target_pairs={{0,48},{1,49},{2,50},{3,51},{4,52},{5,53},{6,54},{7,55},{8,56},{9,... | collective-permute-start | bytes 835592 | tf_op jit(solution)/shard_map/ppermute | solution.py:241
  67.0 11.5 %collective-permute-start.11 = (f32[34,16,128]{2,1,0:T(8,128)S(1)}, f32[34,16,128]{2,1,0:T(8,128)S(1)}, u32[]{:S(2)}, u32[]{:S(2)}) collective-permute-start(f32[34,16,128]{2,1,0:T(8,128)S(1)} %get-tuple-element.57), channel_id=1, source_target_pairs={{0,8},{1,9},{2,10},{3,11},{4,12},{5,13},{6,14},{7,15},{8,0},{9,1},... | collective-permute-start | bytes 835592 | tf_op jit(solution)/shard_map/ppermute | solution.py:241
  68.9 9.5 %collective-permute-start.12 = (bf16[34,16,128]{2,1,0:T(8,128)(2,1)S(1)}, bf16[34,16,128]{2,1,0:T(8,128)(2,1)S(1)}, u32[]{:S(2)}, u32[]{:S(2)}) collective-permute-start(bf16[34,16,128]{2,1,0:T(8,128)(2,1)S(1)} %get-tuple-element.58), channel_id=1, source_target_pairs={{0,8},{1,9},{2,10},{3,11},{4,12},{5,13},{6,14},{7,15},{8,0},{9,1},... | collective-permute-start | bytes 417800 | tf_op jit(solution)/shard_map/ppermute | solution.py:241
  79.2 7.8 %collective-permute-start.13 = (f32[272,128]{1,0:T(8,128)S(1)}, f32[272,128]{1,0:T(8,128)S(1)}, u32[]{:S(2)}, u32[]{:S(2)}) collective-permute-start(f32[272,128]{1,0:T(8,128)S(1)} %get-tuple-element.60), channel_id=1, source_target_pairs={{0,64},{1,65},{2,66},{3,67},{4,68},{5,69},{6,70},{7,71},{8,72},{9,... | collective-permute-start | bytes 417800 | tf_op jit(solution)/shard_map/ppermute | solution.py:241
  80.7 7.8 %collective-permute-start.14 = (f32[272,128]{1,0:T(8,128)S(1)}, f32[272,128]{1,0:T(8,128)S(1)}, u32[]{:S(2)}, u32[]{:S(2)}) collective-permute-start(f32[272,128]{1,0:T(8,128)S(1)} %get-tuple-element.61), channel_id=1, source_target_pairs={{0,2},{1,3},{2,0},{3,1},{4,6},{5,7},{6,4},{7,5},{8,10},{9,11},{10,... | collective-permute-start | bytes 417800 | tf_op jit(solution)/shard_map/ppermute | solution.py:241
  83.4 5.1 %collective-permute-start.15 = (f32[272,128]{1,0:T(8,128)S(1)}, f32[272,128]{1,0:T(8,128)S(1)}, u32[]{:S(2)}, u32[]{:S(2)}) collective-permute-start(f32[272,128]{1,0:T(8,128)S(1)} %get-tuple-element.62), channel_id=1, source_target_pairs={{0,66},{1,67},{2,64},{3,65},{4,70},{5,71},{6,68},{7,69},{8,74},{9,... | collective-permute-start | bytes 417800 | tf_op jit(solution)/shard_map/ppermute | solution.py:241

commit v2 on v1

--- a/solution.py
+++ b/solution.py
@@ -51,8 +51,8 @@
     return [first, second, x - first - second]
 
 
-def prep_kernel(live_ref, lm_hbm, flux_hbm, pairs_hbm, jones_hbm, out_ref, *refs):
-    lm_ref, flux_ref, pairs_ref, jones_ref, info_ref, sems = refs
+def prep_kernel(live_ref, lm_hbm, flux_hbm, pairs_hbm, jones_hbm, out_hbm, *refs):
+    lm_ref, flux_ref, pairs_ref, jones_ref, info_ref, out_ref, sems, out_sems = refs
     copies = [
         pltpu.make_async_copy(src, dst, sems.at[n])
         for n, (src, dst) in enumerate(
@@ -77,11 +77,16 @@
     copies[0].wait()
     src = lax.axis_index("src")
     first = 2 * (src // 4) + src % 2
+    sent = []
     for d in range(STN):
         cols = pl.ds(pl.multiple_of((d + first) % STN * LANES, LANES), LANES)
         for comp in range(8):
             out_ref[d, 64 * comp : 64 * comp + 64, :] = jones_ref[comp, :, cols]
         out_ref[d, JROWS:ROWS, :] = info_ref[:, cols].astype(jnp.bfloat16)
+        sent.append(pltpu.make_async_copy(out_ref.at[d], out_hbm.at[d], out_sems.at[d]))
+        sent[-1].start()
+    for copy in sent:
+        copy.wait()
 
 
 def acc_at(tile, part):
@@ -250,14 +255,16 @@
         prep_kernel,
         out_shape=jax.ShapeDtypeStruct((STN, ROWS, LANES), jnp.bfloat16),
         in_specs=[SMEM] + [pl.BlockSpec(memory_space=pl.ANY)] * 4,
-        out_specs=VMEM,
+        out_specs=pl.BlockSpec(memory_space=pl.ANY),
         scratch_shapes=[
             pltpu.VMEM((2, STN * LANES), jnp.float32),
             pltpu.VMEM((1, STN * LANES), jnp.float32),
             pltpu.VMEM((2, PAIRS_DEV), jnp.int32),
             pltpu.VMEM((8, 64, STN * LANES), jnp.bfloat16),
             pltpu.VMEM((EXTRA, STN * LANES), jnp.float32),
+            pltpu.VMEM((STN, ROWS, LANES), jnp.bfloat16),
             pltpu.SemaphoreType.DMA((4,)),
+            pltpu.SemaphoreType.DMA((STN,)),
         ],
         compiler_params=ALONE,
     )(live_counts, source_lm, source_flux.reshape(1, -1), block_pairs.T, beam_jones)

time: 91.1 us -> 90.8 us (level)
  no operation moved by 1% of the time
where the time goes in v2:
time: 90.8 us; the launch traced here: 89.2 us
  waiting for transfers between devices  38.6 us (43%)
  starting transfers between devices  25.4 us (28%)
  Pallas kernels  21.5 us (24%)
  local copies, waits for them, and re-layouts  2.25 us (2%)
    ppermute x16, waiting for transfers between devices, move(): return lax.ppermute(x, ('stn', 'src'), perm)  23.6 us
    ppermute x16, starting transfers between devices, move(): return lax.ppermute(x, ('stn', 'src'), perm)  19.9 us
    pallas_call x5, Pallas kernels, slab(): pl.pallas_call(functools.partial(slab_kernel, chan, packs, chained, [len(...  17.3 us
    all_to_all x1, waiting for transfers between devices, body(): own = lax.all_to_all(message, 'stn', 0, 0, tiled=True)  15.1 us
    all_to_all x1, starting transfers between devices, body(): own = lax.all_to_all(message, 'stn', 0, 0, tiled=True)  5.49 us
    pallas_call x1, Pallas kernels, body(): pl.pallas_call(prep_kernel, out_shape=jax.ShapeDtypeStruct((STN, ROWS, LA...  2.38 us
  transfers between devices with their start and end apart: 17, of which 10 were waited for; matrix products, arithmetic and copies ran while one was open for 3% of the time, Pallas kernels for 16%

profile of v2, /device:TPU:0, one launch (start us, length us, event | category | flops | bytes accessed | tf_op | source)
XLA Modules:
  0.0 89.2 jit_solution(2729659072978519729)
XLA Ops:
  0.7 2.4 %shard_map.82 = bf16[8,528,128]{2,1,0:T(8,128)(2,1)} custom-call(s32[1]{0:T(128)S(6)} %copy.13.live_ref, f32[2,1024]{1,0:T(2,128)} %lm_hbm.1, f32[1,1024]{1,0:T(1,128)} %bitcast.16, s32[2,17]{1,0:T(2,128)} %bitcast.17, bf16[8,64,1024]{2,1,0:T(8,128)(2,1)} %jones_hbm.1), custom_call_target="tpu_custom_call" | custom-call | tf_op jit(solution)/shard_map/pallas_call | solution.py:254
  3.0 5.5 %all-to-all-start = ((bf16[8,528,128]{2,1,0:T(8,128)(2,1)}), bf16[8,528,128]{2,1,0:T(8,128)(2,1)S(1)}, u32[]{:S(2)}, u32[]{:S(2)}) async-start(bf16[8,528,128]{2,1,0:T(8,128)(2,1)} %shard_map.82), calls=%async_computation | async-start | bytes 2162688 | tf_op jit(solution)/shard_map/all_to_all | solution.py:272
  8.5 0.1 fusion.7
  8.6 15.1 %all-to-all-done.refs_3_ = bf16[8,528,128]{2,1,0:T(8,128)(2,1)S(1)} async-done(((bf16[8,528,128]{2,1,0:T(8,128)(2,1)}), bf16[8,528,128]{2,1,0:T(8,128)(2,1)S(1)}, u32[]{:S(2)}, u32[]{:S(2)}) %all-to-all-start) | async-done | bytes 1081376 | tf_op jit(solution)/shard_map/all_to_all | solution.py:272
  23.7 0.0 collective-permute-start
  23.7 0.1 pad_add_fusion.refs_1_.int_ref
  23.8 0.1 add.189
  23.9 0.1 reshape.406
  24.0 0.1 fusion.2
  24.1 0.0 copy-start.2
  24.1 0.0 copy-start.1
  24.1 1.1 %fusion.8 = (bf16[4,528,128]{2,1,0:T(8,128)(2,1)}, bf16[4,528,128]{2,1,0:T(8,128)(2,1)}) fusion(bf16[8,528,128]{2,1,0:T(8,128)(2,1)S(1)} %all-to-all-done.refs_3_), kind=kLoop, calls=%fused_computation.36 | loop fusion | bytes 2162688 | tf_op jit(solution)/shard_map/slice | solution.py:273
  25.2 1.9 %collective-permute-start.2 = (bf16[4,528,128]{2,1,0:T(8,128)(2,1)}, bf16[4,528,128]{2,1,0:T(8,128)(2,1)S(1)}, u32[]{:S(2)}, u32[]{:S(2)}) collective-permute-start(bf16[4,528,128]{2,1,0:T(8,128)(2,1)} %get-tuple-element.63), channel_id=1, source_target_pairs={{0,4},{1,13},{2,6},{3,15},{4,8},{5,1},{6,10},{7,3},{8,12},{9,5},{1... | collective-permute-start | bytes 1622024 | tf_op jit(solution)/shard_map/ppermute | solution.py:246
  27.1 1.9 %collective-permute-start.1 = (bf16[4,528,128]{2,1,0:T(8,128)(2,1)}, bf16[4,528,128]{2,1,0:T(8,128)(2,1)S(1)}, u32[]{:S(2)}, u32[]{:S(2)}) collective-permute-start(bf16[4,528,128]{2,1,0:T(8,128)(2,1)} %get-tuple-element.64), channel_id=1, source_target_pairs={{0,4},{1,13},{2,6},{3,15},{4,8},{5,1},{6,10},{7,3},{8,12},{9,5},{1... | collective-permute-start | bytes 1622024 | tf_op jit(solution)/shard_map/ppermute | solution.py:246
  29.0 0.0 collective-permute-done.refs_4_
  29.1 0.1 add.177
  29.1 0.0 copy-done.2
  29.1 0.6 gather_fusion
  29.8 0.0 copy-done.1
  29.8 0.3 broadcast_in_dim.46.refs_2_.refs_3_
  30.1 3.7 %shard_map.84.refs_5_ = f32[2560,256]{1,0:T(8,128)S(1)} custom-call(f32[2]{0:T(128)S(1)} %gather_fusion, s32[2]{0:T(128)S(1)} %pad_add_fusion.refs_1_.int_ref, f32[3,512,128]{2,1,0:T(8,128)S(1)} %broadcast_in_dim.46.refs_2_.refs_3_, bf16[8,528,128]{2,1,0:T(8,128)(2,1)S(1)} %all-to-all-done.refs_3_, bf16[8,528,128]{2,1,0:T(8,128)(2,1)S(1)} %collective-permute-done.refs_4_), custom_call_target="tpu_custom_call" | custom-call | tf_op jit(solution)/shard_map/pallas_call | solution.py:296
  33.8 3.7 %shard_map.83.refs_8_ = f32[2560,256]{1,0:T(8,128)S(1)} custom-call(f32[2]{0:T(128)S(1)} %gather_fusion, s32[2]{0:T(128)S(1)} %pad_add_fusion.refs_1_.int_ref, f32[3,512,128]{2,1,0:T(8,128)S(1)} %broadcast_in_dim.46.refs_2_.refs_3_, bf16[8,528,128]{2,1,0:T(8,128)(2,1)S(1)} %all-to-all-done.refs_3_, bf16[8,528,128]{2,1,0:T(8,128)(2,1)S(1)} %collective-permute-done.refs_4_), custom_call_target="tpu_custom_call" | custom-call | tf_op jit(solution)/shard_map/pallas_call | solution.py:296
  37.6 0.0 collective-permute-done.2.refs_4_.refs_5_
  37.6 5.0 %collective-permute-done.1.refs_3_.refs_4_ = bf16[4,528,128]{2,1,0:T(8,128)(2,1)S(1)} collective-permute-done((bf16[4,528,128]{2,1,0:T(8,128)(2,1)}, bf16[4,528,128]{2,1,0:T(8,128)(2,1)S(1)}, u32[]{:S(2)}, u32[]{:S(2)}) %collective-permute-start.1) | collective-permute-done | bytes 540704 | tf_op jit(solution)/shard_map/ppermute | solution.py:246
  42.5 0.0 collective-permute-start.3
  42.5 0.5 collective-permute-start.4
  43.1 0.1 iota_compare_fusion
  43.2 0.2 select_reduce_fusion
  43.3 2.4 %shard_map.85.refs_6_ = f32[2560,256]{1,0:T(8,128)S(1)} custom-call(f32[2]{0:T(128)S(1)} %gather_fusion, s32[2]{0:T(128)S(1)} %pad_add_fusion.refs_1_.int_ref, f32[3,512,128]{2,1,0:T(8,128)S(1)} %broadcast_in_dim.46.refs_2_.refs_3_, bf16[4,528,128]{2,1,0:T(8,128)(2,1)S(1)} %collective-permute-done.1.refs_3_.refs_4_, ...), custom_call_target="tpu_custom_call", output_to_operand_aliasing={{}: (5, {})} | custom-call | tf_op jit(solution)/shard_map/pallas_call | solution.py:296
  45.8 0.0 collective-permute-done.3.refs_4_.refs_6_
  45.8 0.0 collective-permute-done.4.refs_5_.refs_7_
  45.8 3.0 %shard_map.86 = (bf16[68,16,128]{2,1,0:T(8,128)(2,1)S(1)}, bf16[68,16,128]{2,1,0:T(8,128)(2,1)S(1)}, bf16[68,16,128]{2,1,0:T(8,128)(2,1)S(1)}, bf16[68,16,128]{2,1,0:T(8,128)(2,1)S(1)}) custom-call(f32[2]{0:T(128)S(1)} %gather_fusion, s32[2]{0:T(128)S(1)} %pad_add_fusion.refs_1_.int_ref, s32[512]{0:T(512)S(1)} %bitcast.14, ...), custom_call_target="tpu_custom_call" | custom-call | tf_op jit(solution)/shard_map/pallas_call | solution.py:296
  48.8 0.9 %collective-permute-start.8 = (bf16[68,16,128]{2,1,0:T(8,128)(2,1)S(1)}, bf16[68,16,128]{2,1,0:T(8,128)(2,1)S(1)}, u32[]{:S(2)}, u32[]{:S(2)}) collective-permute-start(bf16[68,16,128]{2,1,0:T(8,128)(2,1)S(1)} %get-tuple-element.54), channel_id=1, source_target_pairs={{0,16},{1,17},{2,18},{3,19},{4,20},{5,21},{6,22},{7,23},{8,24},{9,... | collective-permute-start | bytes 835592 | tf_op jit(solution)/shard_map/ppermute | solution.py:246
  49.7 2.1 %collective-permute-start.9 = (bf16[68,16,128]{2,1,0:T(8,128)(2,1)S(1)}, bf16[68,16,128]{2,1,0:T(8,128)(2,1)S(1)}, u32[]{:S(2)}, u32[]{:S(2)}) collective-permute-start(bf16[68,16,128]{2,1,0:T(8,128)(2,1)S(1)} %get-tuple-element.55), channel_id=1, source_target_pairs={{0,32},{1,33},{2,34},{3,35},{4,36},{5,37},{6,38},{7,39},{8,40},{9,... | collective-permute-start | bytes 835592 | tf_op jit(solution)/shard_map/ppermute | solution.py:246
  51.8 1.5 %collective-permute-start.10 = (bf16[68,16,128]{2,1,0:T(8,128)(2,1)S(1)}, bf16[68,16,128]{2,1,0:T(8,128)(2,1)S(1)}, u32[]{:S(2)}, u32[]{:S(2)}) collective-permute-start(bf16[68,16,128]{2,1,0:T(8,128)(2,1)S(1)} %get-tuple-element.56), channel_id=1, source_target_pairs={{0,48},{1,49},{2,50},{3,51},{4,52},{5,53},{6,54},{7,55},{8,56},{9,... | collective-permute-start | bytes 835592 | tf_op jit(solution)/shard_map/ppermute | solution.py:246
  53.3 4.4 %shard_map.87 = (bf16[68,16,128]{2,1,0:T(8,128)(2,1)S(1)}, bf16[68,16,128]{2,1,0:T(8,128)(2,1)S(1)}, bf16[68,16,128]{2,1,0:T(8,128)(2,1)S(1)}, bf16[68,16,128]{2,1,0:T(8,128)(2,1)S(1)}) custom-call(f32[2]{0:T(128)S(1)} %gather_fusion, s32[2]{0:T(128)S(1)} %pad_add_fusion.refs_1_.int_ref, s32[512]{0:T(512)S(1)} %bitcast.15, ...), custom_call_target="tpu_custom_call" | custom-call | tf_op jit(solution)/shard_map/pallas_call | solution.py:296
  57.7 0.6 collective-permute-start.5
  58.3 1.4 %collective-permute-start.6 = (bf16[68,16,128]{2,1,0:T(8,128)(2,1)S(1)}, bf16[68,16,128]{2,1,0:T(8,128)(2,1)S(1)}, u32[]{:S(2)}, u32[]{:S(2)}) collective-permute-start(bf16[68,16,128]{2,1,0:T(8,128)(2,1)S(1)} %get-tuple-element.51), channel_id=1, source_target_pairs={{0,32},{1,33},{2,34},{3,35},{4,36},{5,37},{6,38},{7,39},{8,40},{9,... | collective-permute-start | bytes 835592 | tf_op jit(solution)/shard_map/ppermute | solution.py:246
  59.7 4.5 %collective-permute-done.8.two = bf16[68,16,128]{2,1,0:T(8,128)(2,1)S(1)} collective-permute-done((bf16[68,16,128]{2,1,0:T(8,128)(2,1)S(1)}, bf16[68,16,128]{2,1,0:T(8,128)(2,1)S(1)}, u32[]{:S(2)}, u32[]{:S(2)}) %collective-permute-start.8) | collective-permute-done | bytes 278560 | tf_op jit(solution)/shard_map/ppermute | solution.py:246
  64.2 0.0 copy-start
  64.2 0.0 collective-permute-start.7
  64.2 1.1 %collective-permute-done.9.three = bf16[68,16,128]{2,1,0:T(8,128)(2,1)S(1)} collective-permute-done((bf16[68,16,128]{2,1,0:T(8,128)(2,1)S(1)}, bf16[68,16,128]{2,1,0:T(8,128)(2,1)S(1)}, u32[]{:S(2)}, u32[]{:S(2)}) %collective-permute-start.9) | collective-permute-done | bytes 278560 | tf_op jit(solution)/shard_map/ppermute | solution.py:246
  65.3 1.2 %collective-permute-done.10.four = bf16[68,16,128]{2,1,0:T(8,128)(2,1)S(1)} collective-permute-done((bf16[68,16,128]{2,1,0:T(8,128)(2,1)S(1)}, bf16[68,16,128]{2,1,0:T(8,128)(2,1)S(1)}, u32[]{:S(2)}, u32[]{:S(2)}) %collective-permute-start.10) | collective-permute-done | bytes 278560 | tf_op jit(solution)/shard_map/ppermute | solution.py:246
  66.5 0.1 shard_map.88
  66.6 2.0 %collective-permute-start.11 = (f32[34,16,128]{2,1,0:T(8,128)S(1)}, f32[34,16,128]{2,1,0:T(8,128)S(1)}, u32[]{:S(2)}, u32[]{:S(2)}) collective-permute-start(f32[34,16,128]{2,1,0:T(8,128)S(1)} %get-tuple-element.57), channel_id=1, source_target_pairs={{0,8},{1,9},{2,10},{3,11},{4,12},{5,13},{6,14},{7,15},{8,0},{9,1},... | collective-permute-start | bytes 835592 | tf_op jit(solution)/shard_map/ppermute | solution.py:246
  68.6 1.6 %collective-permute-start.12 = (bf16[34,16,128]{2,1,0:T(8,128)(2,1)S(1)}, bf16[34,16,128]{2,1,0:T(8,128)(2,1)S(1)}, u32[]{:S(2)}, u32[]{:S(2)}) collective-permute-start(bf16[34,16,128]{2,1,0:T(8,128)(2,1)S(1)} %get-tuple-element.58), channel_id=1, source_target_pairs={{0,8},{1,9},{2,10},{3,11},{4,12},{5,13},{6,14},{7,15},{8,0},{9,1},... | collective-permute-start | bytes 417800 | tf_op jit(solution)/shard_map/ppermute | solution.py:246
  70.2 6.4 %collective-permute-done.5.two = bf16[68,16,128]{2,1,0:T(8,128)(2,1)S(1)} collective-permute-done((bf16[68,16,128]{2,1,0:T(8,128)(2,1)S(1)}, bf16[68,16,128]{2,1,0:T(8,128)(2,1)S(1)}, u32[]{:S(2)}, u32[]{:S(2)}) %collective-permute-start.5) | collective-permute-done | bytes 278560 | tf_op jit(solution)/shard_map/ppermute | solution.py:246
  76.6 0.0 collective-permute-done.6.three
  76.6 0.7 collective-permute-done.7.four
  77.3 0.8 collective-permute-done.12.imag_ref
  78.1 0.0 collective-permute-done.11.real_ref
  78.1 0.7 shard_map.89
  78.8 1.5 %collective-permute-start.13 = (f32[272,128]{1,0:T(8,128)S(1)}, f32[272,128]{1,0:T(8,128)S(1)}, u32[]{:S(2)}, u32[]{:S(2)}) collective-permute-start(f32[272,128]{1,0:T(8,128)S(1)} %get-tuple-element.60), channel_id=1, source_target_pairs={{0,64},{1,65},{2,66},{3,67},{4,68},{5,69},{6,70},{7,71},{8,72},{9,... | collective-permute-start | bytes 417800 | tf_op jit(solution)/shard_map/ppermute | solution.py:246
  80.4 2.7 %collective-permute-start.14 = (f32[272,128]{1,0:T(8,128)S(1)}, f32[272,128]{1,0:T(8,128)S(1)}, u32[]{:S(2)}, u32[]{:S(2)}) collective-permute-start(f32[272,128]{1,0:T(8,128)S(1)} %get-tuple-element.61), channel_id=1, source_target_pairs={{0,2},{1,3},{2,0},{3,1},{4,6},{5,7},{6,4},{7,5},{8,10},{9,11},{10,... | collective-permute-start | bytes 417800 | tf_op jit(solution)/shard_map/ppermute | solution.py:246
  83.1 1.2 %collective-permute-start.15 = (f32[272,128]{1,0:T(8,128)S(1)}, f32[272,128]{1,0:T(8,128)S(1)}, u32[]{:S(2)}, u32[]{:S(2)}) collective-permute-start(f32[272,128]{1,0:T(8,128)S(1)} %get-tuple-element.62), channel_id=1, source_target_pairs={{0,66},{1,67},{2,64},{3,65},{4,70},{5,71},{6,68},{7,69},{8,74},{9,... | collective-permute-start | bytes 417800 | tf_op jit(solution)/shard_map/ppermute | solution.py:246
  84.3 2.4 %collective-permute-done.13.refs_1_ = f32[272,128]{1,0:T(8,128)S(1)} collective-permute-done((f32[272,128]{1,0:T(8,128)S(1)}, f32[272,128]{1,0:T(8,128)S(1)}, u32[]{:S(2)}, u32[]{:S(2)}) %collective-permute-start.13) | collective-permute-done | bytes 139296 | tf_op jit(solution)/shard_map/ppermute | solution.py:246
  86.7 1.6 %collective-permute-done.14.refs_2_ = f32[272,128]{1,0:T(8,128)S(1)} collective-permute-done((f32[272,128]{1,0:T(8,128)S(1)}, f32[272,128]{1,0:T(8,128)S(1)}, u32[]{:S(2)}, u32[]{:S(2)}) %collective-permute-start.14) | collective-permute-done | bytes 139296 | tf_op jit(solution)/shard_map/ppermute | solution.py:246
  88.2 0.0 collective-permute-done.15.refs_3_
  88.2 0.0 copy-done
  88.2 1.0 %shard_map.90 = f32[17,2048]{1,0:T(8,128)} custom-call(f32[272,128]{1,0:T(8,128)S(1)} %get-tuple-element.59.refs_0_, f32[272,128]{1,0:T(8,128)S(1)} %collective-permute-done.13.refs_1_, f32[272,128]{1,0:T(8,128)S(1)} %collective-permute-done.14.refs_2_, f32[272,128]{1,0:T(8,128)S(1)} %collective-permute-done.15.refs_3_, f32[128,128]{1,0:T(8,128)S(1)} %copy-done), custom_call_target="tpu_custom_call" | custom-call | tf_op jit(solution)/shard_map/pallas_call | solution.py:335
  (12 shorter events, 0.1 us)
Async XLA Ops:
  3.0 20.6 %all-to-all-start = ((bf16[8,528,128]{2,1,0:T(8,128)(2,1)}), bf16[8,528,128]{2,1,0:T(8,128)(2,1)S(1)}, u32[]{:S(2)}, u32[]{:S(2)}) async-start(bf16[8,528,128]{2,1,0:T(8,128)(2,1)} %shard_map.82), calls=%async_computation | async-start | bytes 2162688 | tf_op jit(solution)/shard_map/all_to_all | solution.py:272
  23.7 5.3 %collective-permute-start = (bf16[8,528,128]{2,1,0:T(8,128)(2,1)S(1)}, bf16[8,528,128]{2,1,0:T(8,128)(2,1)S(1)}, u32[]{:S(2)}, u32[]{:S(2)}) collective-permute-start(bf16[8,528,128]{2,1,0:T(8,128)(2,1)S(1)} %all-to-all-done.refs_3_), channel_id=1, source_target_pairs={{0,1},{1,0},{2,3},{3,2},{4,5},{5,4},{6,7},{7,6},{8,9},{9,8},{10,11... | collective-permute-start | bytes 3244040 | tf_op jit(solution)/shard_map/ppermute | solution.py:246
  24.1 5.1 %copy-start.2 = (f32[4]{0:T(128)S(1)}, f32[4]{0:T(128)}, u32[]{:S(2)}) copy-start(f32[4]{0:T(128)} %param.13) | copy-start | bytes 52
  24.1 5.7 %copy-start.1 = (f32[3,512]{1,0:T(4,128)S(1)}, f32[3,512]{1,0:T(4,128)}, u32[]{:S(2)}) copy-start(f32[3,512]{1,0:T(4,128)} %param.12) | copy-start | bytes 18436
  25.2 12.4 %collective-permute-start.2 = (bf16[4,528,128]{2,1,0:T(8,128)(2,1)}, bf16[4,528,128]{2,1,0:T(8,128)(2,1)S(1)}, u32[]{:S(2)}, u32[]{:S(2)}) collective-permute-start(bf16[4,528,128]{2,1,0:T(8,128)(2,1)} %get-tuple-element.63), channel_id=1, source_target_pairs={{0,4},{1,13},{2,6},{3,15},{4,8},{5,1},{6,10},{7,3},{8,12},{9,5},{1... | collective-permute-start | bytes 1622024 | tf_op jit(solution)/shard_map/ppermute | solution.py:246
  27.1 15.5 %collective-permute-start.1 = (bf16[4,528,128]{2,1,0:T(8,128)(2,1)}, bf16[4,528,128]{2,1,0:T(8,128)(2,1)S(1)}, u32[]{:S(2)}, u32[]{:S(2)}) collective-permute-start(bf16[4,528,128]{2,1,0:T(8,128)(2,1)} %get-tuple-element.64), channel_id=1, source_target_pairs={{0,4},{1,13},{2,6},{3,15},{4,8},{5,1},{6,10},{7,3},{8,12},{9,5},{1... | collective-permute-start | bytes 1622024 | tf_op jit(solution)/shard_map/ppermute | solution.py:246
  42.5 3.2 %collective-permute-start.3 = (bf16[4,528,128]{2,1,0:T(8,128)(2,1)S(1)}, bf16[4,528,128]{2,1,0:T(8,128)(2,1)S(1)}, u32[]{:S(2)}, u32[]{:S(2)}) collective-permute-start(bf16[4,528,128]{2,1,0:T(8,128)(2,1)S(1)} %collective-permute-done.1.refs_3_.refs_4_), channel_id=1, source_target_pairs={{0,1},{1,0},{2,3},{3,2},{4,5},{5,4},{6,7},{7,6},{8,9},{9,8},{10,11... | collective-permute-start | bytes 1622024 | tf_op jit(solution)/shard_map/ppermute | solution.py:246
  42.5 3.2 %collective-permute-start.4 = (bf16[4,528,128]{2,1,0:T(8,128)(2,1)S(1)}, bf16[4,528,128]{2,1,0:T(8,128)(2,1)S(1)}, u32[]{:S(2)}, u32[]{:S(2)}) collective-permute-start(bf16[4,528,128]{2,1,0:T(8,128)(2,1)S(1)} %collective-permute-done.2.refs_4_.refs_5_), channel_id=1, source_target_pairs={{0,1},{1,0},{2,3},{3,2},{4,5},{5,4},{6,7},{7,6},{8,9},{9,8},{10,11... | collective-permute-start | bytes 1622024 | tf_op jit(solution)/shard_map/ppermute | solution.py:246
  48.8 15.4 %collective-permute-start.8 = (bf16[68,16,128]{2,1,0:T(8,128)(2,1)S(1)}, bf16[68,16,128]{2,1,0:T(8,128)(2,1)S(1)}, u32[]{:S(2)}, u32[]{:S(2)}) collective-permute-start(bf16[68,16,128]{2,1,0:T(8,128)(2,1)S(1)} %get-tuple-element.54), channel_id=1, source_target_pairs={{0,16},{1,17},{2,18},{3,19},{4,20},{5,21},{6,22},{7,23},{8,24},{9,... | collective-permute-start | bytes 835592 | tf_op jit(solution)/shard_map/ppermute | solution.py:246
  49.7 15.6 %collective-permute-start.9 = (bf16[68,16,128]{2,1,0:T(8,128)(2,1)S(1)}, bf16[68,16,128]{2,1,0:T(8,128)(2,1)S(1)}, u32[]{:S(2)}, u32[]{:S(2)}) collective-permute-start(bf16[68,16,128]{2,1,0:T(8,128)(2,1)S(1)} %get-tuple-element.55), channel_id=1, source_target_pairs={{0,32},{1,33},{2,34},{3,35},{4,36},{5,37},{6,38},{7,39},{8,40},{9,... | collective-permute-start | bytes 835592 | tf_op jit(solution)/shard_map/ppermute | solution.py:246
  51.8 14.7 %collective-permute-start.10 = (bf16[68,16,128]{2,1,0:T(8,128)(2,1)S(1)}, bf16[68,16,128]{2,1,0:T(8,128)(2,1)S(1)}, u32[]{:S(2)}, u32[]{:S(2)}) collective-permute-start(bf16[68,16,128]{2,1,0:T(8,128)(2,1)S(1)} %get-tuple-element.56), channel_id=1, source_target_pairs={{0,48},{1,49},{2,50},{3,51},{4,52},{5,53},{6,54},{7,55},{8,56},{9,... | collective-permute-start | bytes 835592 | tf_op jit(solution)/shard_map/ppermute | solution.py:246
  57.7 18.9 %collective-permute-start.5 = (bf16[68,16,128]{2,1,0:T(8,128)(2,1)S(1)}, bf16[68,16,128]{2,1,0:T(8,128)(2,1)S(1)}, u32[]{:S(2)}, u32[]{:S(2)}) collective-permute-start(bf16[68,16,128]{2,1,0:T(8,128)(2,1)S(1)} %get-tuple-element.50), channel_id=1, source_target_pairs={{0,16},{1,17},{2,18},{3,19},{4,20},{5,21},{6,22},{7,23},{8,24},{9,... | collective-permute-start | bytes 835592 | tf_op jit(solution)/shard_map/ppermute | solution.py:246
  58.3 18.3 %collective-permute-start.6 = (bf16[68,16,128]{2,1,0:T(8,128)(2,1)S(1)}, bf16[68,16,128]{2,1,0:T(8,128)(2,1)S(1)}, u32[]{:S(2)}, u32[]{:S(2)}) collective-permute-start(bf16[68,16,128]{2,1,0:T(8,128)(2,1)S(1)} %get-tuple-element.51), channel_id=1, source_target_pairs={{0,32},{1,33},{2,34},{3,35},{4,36},{5,37},{6,38},{7,39},{8,40},{9,... | collective-permute-start | bytes 835592 | tf_op jit(solution)/shard_map/ppermute | solution.py:246
  64.2 24.0 %copy-start = (f32[128,128]{1,0:T(8,128)S(1)}, f32[128,128]{1,0:T(8,128)}, u32[]{:S(2)}) copy-start(f32[128,128]{1,0:T(8,128)} %constant.111.clone.refs_4_) | copy-start | bytes 196612
  64.2 13.1 %collective-permute-start.7 = (bf16[68,16,128]{2,1,0:T(8,128)(2,1)S(1)}, bf16[68,16,128]{2,1,0:T(8,128)(2,1)S(1)}, u32[]{:S(2)}, u32[]{:S(2)}) collective-permute-start(bf16[68,16,128]{2,1,0:T(8,128)(2,1)S(1)} %get-tuple-element.52), channel_id=1, source_target_pairs={{0,48},{1,49},{2,50},{3,51},{4,52},{5,53},{6,54},{7,55},{8,56},{9,... | collective-permute-start | bytes 835592 | tf_op jit(solution)/shard_map/ppermute | solution.py:246
  66.6 11.5 %collective-permute-start.11 = (f32[34,16,128]{2,1,0:T(8,128)S(1)}, f32[34,16,128]{2,1,0:T(8,128)S(1)}, u32[]{:S(2)}, u32[]{:S(2)}) collective-permute-start(f32[34,16,128]{2,1,0:T(8,128)S(1)} %get-tuple-element.57), channel_id=1, source_target_pairs={{0,8},{1,9},{2,10},{3,11},{4,12},{5,13},{6,14},{7,15},{8,0},{9,1},... | collective-permute-start | bytes 835592 | tf_op jit(solution)/shard_map/ppermute | solution.py:246
  68.6 9.5 %collective-permute-start.12 = (bf16[34,16,128]{2,1,0:T(8,128)(2,1)S(1)}, bf16[34,16,128]{2,1,0:T(8,128)(2,1)S(1)}, u32[]{:S(2)}, u32[]{:S(2)}) collective-permute-start(bf16[34,16,128]{2,1,0:T(8,128)(2,1)S(1)} %get-tuple-element.58), channel_id=1, source_target_pairs={{0,8},{1,9},{2,10},{3,11},{4,12},{5,13},{6,14},{7,15},{8,0},{9,1},... | collective-permute-start | bytes 417800 | tf_op jit(solution)/shard_map/ppermute | solution.py:246
  78.8 7.8 %collective-permute-start.13 = (f32[272,128]{1,0:T(8,128)S(1)}, f32[272,128]{1,0:T(8,128)S(1)}, u32[]{:S(2)}, u32[]{:S(2)}) collective-permute-start(f32[272,128]{1,0:T(8,128)S(1)} %get-tuple-element.60), channel_id=1, source_target_pairs={{0,64},{1,65},{2,66},{3,67},{4,68},{5,69},{6,70},{7,71},{8,72},{9,... | collective-permute-start | bytes 417800 | tf_op jit(solution)/shard_map/ppermute | solution.py:246
  80.4 7.9 %collective-permute-start.14 = (f32[272,128]{1,0:T(8,128)S(1)}, f32[272,128]{1,0:T(8,128)S(1)}, u32[]{:S(2)}, u32[]{:S(2)}) collective-permute-start(f32[272,128]{1,0:T(8,128)S(1)} %get-tuple-element.61), channel_id=1, source_target_pairs={{0,2},{1,3},{2,0},{3,1},{4,6},{5,7},{6,4},{7,5},{8,10},{9,11},{10,... | collective-permute-start | bytes 417800 | tf_op jit(solution)/shard_map/ppermute | solution.py:246
  83.1 5.1 %collective-permute-start.15 = (f32[272,128]{1,0:T(8,128)S(1)}, f32[272,128]{1,0:T(8,128)S(1)}, u32[]{:S(2)}, u32[]{:S(2)}) collective-permute-start(f32[272,128]{1,0:T(8,128)S(1)} %get-tuple-element.62), channel_id=1, source_target_pairs={{0,66},{1,67},{2,64},{3,65},{4,70},{5,71},{6,68},{7,69},{8,74},{9,... | collective-permute-start | bytes 417800 | tf_op jit(solution)/shard_map/ppermute | solution.py:246

commit v3 on v2

--- a/solution.py
+++ b/solution.py
@@ -306,7 +306,8 @@
         )(scale, ints, *([index[chan]] if packs else []), uvw, *flat, *([before] if chained else []))
 
     def along_y(shares):
-        return [shares[0]] + [move(shares[n], dy=n) for n in (1, 2, 3)]
+        moved = {n: move(shares[n], dy=n) for n in (2, 1, 3)}
+        return [shares[0]] + [moved[n] for n in (1, 2, 3)]
 
     far = slab(1, False, [[own], [other]])
     near = slab(0, False, [[own], [other]])
@@ -327,7 +328,7 @@
         add_near_kernel, out_shape=[small] * 4, in_specs=[SMEM] + [VMEM] * 6, out_specs=[VMEM] * 4,
         compiler_params=PARAMS,
     )(ints, *along_y(near), move(real, dz=2), move(imag, dz=2))
-    near = [near[0]] + [move(near[n], dx=n) for n in (1, 2, 3)]
+    near = [near[0]] + [move(near[n], dx=n) for n in (2, 1, 3)]
 
     lane = np.arange(LANES)
     order = np.zeros((LANES, LANES), np.float32)

time: 90.8 us -> 90.9 us (level)
  no operation moved by 1% of the time
where the time goes in v3:
time: 90.9 us; the launch traced here: 89.2 us
  waiting for transfers between devices  38 us (42%)
  starting transfers between devices  26 us (29%)
  Pallas kernels  21.5 us (24%)
  local copies, waits for them, and re-layouts  2.25 us (2%)
    ppermute x16, waiting for transfers between devices, move(): return lax.ppermute(x, ('stn', 'src'), perm)  22.9 us
    ppermute x16, starting transfers between devices, move(): return lax.ppermute(x, ('stn', 'src'), perm)  20.6 us
    pallas_call x5, Pallas kernels, slab(): pl.pallas_call(functools.partial(slab_kernel, chan, packs, chained, [len(...  17.3 us
    all_to_all x1, waiting for transfers between devices, body(): own = lax.all_to_all(message, 'stn', 0, 0, tiled=True)  15.1 us
    all_to_all x1, starting transfers between devices, body(): own = lax.all_to_all(message, 'stn', 0, 0, tiled=True)  5.49 us
    pallas_call x1, Pallas kernels, body(): pl.pallas_call(prep_kernel, out_shape=jax.ShapeDtypeStruct((STN, ROWS, LA...  2.38 us
  transfers between devices with their start and end apart: 17, of which 10 were waited for; matrix products, arithmetic and copies ran while one was open for 3% of the time, Pallas kernels for 16%

profile of v3, /device:TPU:0, one launch (start us, length us, event | category | flops | bytes accessed | tf_op | source)
XLA Modules:
  0.0 89.2 jit_solution(16450946575761906696)
XLA Ops:
  0.7 2.4 %shard_map.82 = bf16[8,528,128]{2,1,0:T(8,128)(2,1)} custom-call(s32[1]{0:T(128)S(6)} %copy.13.live_ref, f32[2,1024]{1,0:T(2,128)} %lm_hbm.1, f32[1,1024]{1,0:T(1,128)} %bitcast.16, s32[2,17]{1,0:T(2,128)} %bitcast.17, bf16[8,64,1024]{2,1,0:T(8,128)(2,1)} %jones_hbm.1), custom_call_target="tpu_custom_call" | custom-call | tf_op jit(solution)/shard_map/pallas_call | solution.py:254
  3.0 5.5 %all-to-all-start = ((bf16[8,528,128]{2,1,0:T(8,128)(2,1)}), bf16[8,528,128]{2,1,0:T(8,128)(2,1)S(1)}, u32[]{:S(2)}, u32[]{:S(2)}) async-start(bf16[8,528,128]{2,1,0:T(8,128)(2,1)} %shard_map.82), calls=%async_computation | async-start | bytes 2162688 | tf_op jit(solution)/shard_map/all_to_all | solution.py:272
  8.5 0.1 fusion.7
  8.6 15.1 %all-to-all-done.refs_3_ = bf16[8,528,128]{2,1,0:T(8,128)(2,1)S(1)} async-done(((bf16[8,528,128]{2,1,0:T(8,128)(2,1)}), bf16[8,528,128]{2,1,0:T(8,128)(2,1)S(1)}, u32[]{:S(2)}, u32[]{:S(2)}) %all-to-all-start) | async-done | bytes 1081376 | tf_op jit(solution)/shard_map/all_to_all | solution.py:272
  23.7 0.0 collective-permute-start
  23.7 0.1 pad_add_fusion.refs_1_.int_ref
  23.8 0.1 add.189
  23.9 0.1 reshape.406
  24.0 0.1 fusion.2
  24.1 0.0 copy-start.2
  24.1 0.0 copy-start.1
  24.1 1.1 %fusion.8 = (bf16[4,528,128]{2,1,0:T(8,128)(2,1)}, bf16[4,528,128]{2,1,0:T(8,128)(2,1)}) fusion(bf16[8,528,128]{2,1,0:T(8,128)(2,1)S(1)} %all-to-all-done.refs_3_), kind=kLoop, calls=%fused_computation.36 | loop fusion | bytes 2162688 | tf_op jit(solution)/shard_map/slice | solution.py:273
  25.2 1.9 %collective-permute-start.2 = (bf16[4,528,128]{2,1,0:T(8,128)(2,1)}, bf16[4,528,128]{2,1,0:T(8,128)(2,1)S(1)}, u32[]{:S(2)}, u32[]{:S(2)}) collective-permute-start(bf16[4,528,128]{2,1,0:T(8,128)(2,1)} %get-tuple-element.63), channel_id=1, source_target_pairs={{0,4},{1,13},{2,6},{3,15},{4,8},{5,1},{6,10},{7,3},{8,12},{9,5},{1... | collective-permute-start | bytes 1622024 | tf_op jit(solution)/shard_map/ppermute | solution.py:246
  27.1 1.9 %collective-permute-start.1 = (bf16[4,528,128]{2,1,0:T(8,128)(2,1)}, bf16[4,528,128]{2,1,0:T(8,128)(2,1)S(1)}, u32[]{:S(2)}, u32[]{:S(2)}) collective-permute-start(bf16[4,528,128]{2,1,0:T(8,128)(2,1)} %get-tuple-element.64), channel_id=1, source_target_pairs={{0,4},{1,13},{2,6},{3,15},{4,8},{5,1},{6,10},{7,3},{8,12},{9,5},{1... | collective-permute-start | bytes 1622024 | tf_op jit(solution)/shard_map/ppermute | solution.py:246
  29.0 0.0 collective-permute-done.refs_4_
  29.1 0.1 add.177
  29.1 0.0 copy-done.2
  29.1 0.6 gather_fusion
  29.8 0.0 copy-done.1
  29.8 0.3 broadcast_in_dim.46.refs_2_.refs_3_
  30.1 3.7 %shard_map.84.refs_5_ = f32[2560,256]{1,0:T(8,128)S(1)} custom-call(f32[2]{0:T(128)S(1)} %gather_fusion, s32[2]{0:T(128)S(1)} %pad_add_fusion.refs_1_.int_ref, f32[3,512,128]{2,1,0:T(8,128)S(1)} %broadcast_in_dim.46.refs_2_.refs_3_, bf16[8,528,128]{2,1,0:T(8,128)(2,1)S(1)} %all-to-all-done.refs_3_, bf16[8,528,128]{2,1,0:T(8,128)(2,1)S(1)} %collective-permute-done.refs_4_), custom_call_target="tpu_custom_call" | custom-call | tf_op jit(solution)/shard_map/pallas_call | solution.py:296
  33.8 3.7 %shard_map.83.refs_8_ = f32[2560,256]{1,0:T(8,128)S(1)} custom-call(f32[2]{0:T(128)S(1)} %gather_fusion, s32[2]{0:T(128)S(1)} %pad_add_fusion.refs_1_.int_ref, f32[3,512,128]{2,1,0:T(8,128)S(1)} %broadcast_in_dim.46.refs_2_.refs_3_, bf16[8,528,128]{2,1,0:T(8,128)(2,1)S(1)} %all-to-all-done.refs_3_, bf16[8,528,128]{2,1,0:T(8,128)(2,1)S(1)} %collective-permute-done.refs_4_), custom_call_target="tpu_custom_call" | custom-call | tf_op jit(solution)/shard_map/pallas_call | solution.py:296
  37.6 0.0 collective-permute-done.2.refs_4_.refs_5_
  37.6 5.0 %collective-permute-done.1.refs_3_.refs_4_ = bf16[4,528,128]{2,1,0:T(8,128)(2,1)S(1)} collective-permute-done((bf16[4,528,128]{2,1,0:T(8,128)(2,1)}, bf16[4,528,128]{2,1,0:T(8,128)(2,1)S(1)}, u32[]{:S(2)}, u32[]{:S(2)}) %collective-permute-start.1) | collective-permute-done | bytes 540704 | tf_op jit(solution)/shard_map/ppermute | solution.py:246
  42.5 0.0 collective-permute-start.3
  42.5 0.5 collective-permute-start.4
  43.1 0.1 iota_compare_fusion
  43.2 0.2 select_reduce_fusion
  43.3 2.4 %shard_map.85.refs_6_ = f32[2560,256]{1,0:T(8,128)S(1)} custom-call(f32[2]{0:T(128)S(1)} %gather_fusion, s32[2]{0:T(128)S(1)} %pad_add_fusion.refs_1_.int_ref, f32[3,512,128]{2,1,0:T(8,128)S(1)} %broadcast_in_dim.46.refs_2_.refs_3_, bf16[4,528,128]{2,1,0:T(8,128)(2,1)S(1)} %collective-permute-done.1.refs_3_.refs_4_, ...), custom_call_target="tpu_custom_call", output_to_operand_aliasing={{}: (5, {})} | custom-call | tf_op jit(solution)/shard_map/pallas_call | solution.py:296
  45.8 0.0 collective-permute-done.3.refs_4_.refs_6_
  45.8 0.0 collective-permute-done.4.refs_5_.refs_7_
  45.8 3.0 %shard_map.86 = (bf16[68,16,128]{2,1,0:T(8,128)(2,1)S(1)}, bf16[68,16,128]{2,1,0:T(8,128)(2,1)S(1)}, bf16[68,16,128]{2,1,0:T(8,128)(2,1)S(1)}, bf16[68,16,128]{2,1,0:T(8,128)(2,1)S(1)}) custom-call(f32[2]{0:T(128)S(1)} %gather_fusion, s32[2]{0:T(128)S(1)} %pad_add_fusion.refs_1_.int_ref, s32[512]{0:T(512)S(1)} %bitcast.14, ...), custom_call_target="tpu_custom_call" | custom-call | tf_op jit(solution)/shard_map/pallas_call | solution.py:296
  48.8 0.9 %collective-permute-start.8 = (bf16[68,16,128]{2,1,0:T(8,128)(2,1)S(1)}, bf16[68,16,128]{2,1,0:T(8,128)(2,1)S(1)}, u32[]{:S(2)}, u32[]{:S(2)}) collective-permute-start(bf16[68,16,128]{2,1,0:T(8,128)(2,1)S(1)} %get-tuple-element.54), channel_id=1, source_target_pairs={{0,16},{1,17},{2,18},{3,19},{4,20},{5,21},{6,22},{7,23},{8,24},{9,... | collective-permute-start | bytes 835592 | tf_op jit(solution)/shard_map/ppermute | solution.py:246
  49.7 2.1 %collective-permute-start.9 = (bf16[68,16,128]{2,1,0:T(8,128)(2,1)S(1)}, bf16[68,16,128]{2,1,0:T(8,128)(2,1)S(1)}, u32[]{:S(2)}, u32[]{:S(2)}) collective-permute-start(bf16[68,16,128]{2,1,0:T(8,128)(2,1)S(1)} %get-tuple-element.55), channel_id=1, source_target_pairs={{0,32},{1,33},{2,34},{3,35},{4,36},{5,37},{6,38},{7,39},{8,40},{9,... | collective-permute-start | bytes 835592 | tf_op jit(solution)/shard_map/ppermute | solution.py:246
  51.8 1.5 %collective-permute-start.10 = (bf16[68,16,128]{2,1,0:T(8,128)(2,1)S(1)}, bf16[68,16,128]{2,1,0:T(8,128)(2,1)S(1)}, u32[]{:S(2)}, u32[]{:S(2)}) collective-permute-start(bf16[68,16,128]{2,1,0:T(8,128)(2,1)S(1)} %get-tuple-element.56), channel_id=1, source_target_pairs={{0,48},{1,49},{2,50},{3,51},{4,52},{5,53},{6,54},{7,55},{8,56},{9,... | collective-permute-start | bytes 835592 | tf_op jit(solution)/shard_map/ppermute | solution.py:246
  53.3 4.4 %shard_map.87 = (bf16[68,16,128]{2,1,0:T(8,128)(2,1)S(1)}, bf16[68,16,128]{2,1,0:T(8,128)(2,1)S(1)}, bf16[68,16,128]{2,1,0:T(8,128)(2,1)S(1)}, bf16[68,16,128]{2,1,0:T(8,128)(2,1)S(1)}) custom-call(f32[2]{0:T(128)S(1)} %gather_fusion, s32[2]{0:T(128)S(1)} %pad_add_fusion.refs_1_.int_ref, s32[512]{0:T(512)S(1)} %bitcast.15, ...), custom_call_target="tpu_custom_call" | custom-call | tf_op jit(solution)/shard_map/pallas_call | solution.py:296
  57.7 0.6 collective-permute-start.5
  58.3 1.4 %collective-permute-start.6 = (bf16[68,16,128]{2,1,0:T(8,128)(2,1)S(1)}, bf16[68,16,128]{2,1,0:T(8,128)(2,1)S(1)}, u32[]{:S(2)}, u32[]{:S(2)}) collective-permute-start(bf16[68,16,128]{2,1,0:T(8,128)(2,1)S(1)} %get-tuple-element.51), channel_id=1, source_target_pairs={{0,32},{1,33},{2,34},{3,35},{4,36},{5,37},{6,38},{7,39},{8,40},{9,... | collective-permute-start | bytes 835592 | tf_op jit(solution)/shard_map/ppermute | solution.py:246
  59.7 4.5 %collective-permute-done.8.two = bf16[68,16,128]{2,1,0:T(8,128)(2,1)S(1)} collective-permute-done((bf16[68,16,128]{2,1,0:T(8,128)(2,1)S(1)}, bf16[68,16,128]{2,1,0:T(8,128)(2,1)S(1)}, u32[]{:S(2)}, u32[]{:S(2)}) %collective-permute-start.8) | collective-permute-done | bytes 278560 | tf_op jit(solution)/shard_map/ppermute | solution.py:246
  64.2 0.0 copy-start
  64.2 0.0 collective-permute-start.7
  64.2 1.1 %collective-permute-done.9.three = bf16[68,16,128]{2,1,0:T(8,128)(2,1)S(1)} collective-permute-done((bf16[68,16,128]{2,1,0:T(8,128)(2,1)S(1)}, bf16[68,16,128]{2,1,0:T(8,128)(2,1)S(1)}, u32[]{:S(2)}, u32[]{:S(2)}) %collective-permute-start.9) | collective-permute-done | bytes 278560 | tf_op jit(solution)/shard_map/ppermute | solution.py:246
  65.3 1.2 %collective-permute-done.10.four = bf16[68,16,128]{2,1,0:T(8,128)(2,1)S(1)} collective-permute-done((bf16[68,16,128]{2,1,0:T(8,128)(2,1)S(1)}, bf16[68,16,128]{2,1,0:T(8,128)(2,1)S(1)}, u32[]{:S(2)}, u32[]{:S(2)}) %collective-permute-start.10) | collective-permute-done | bytes 278560 | tf_op jit(solution)/shard_map/ppermute | solution.py:246
  66.5 0.1 shard_map.88
  66.6 2.0 %collective-permute-start.11 = (f32[34,16,128]{2,1,0:T(8,128)S(1)}, f32[34,16,128]{2,1,0:T(8,128)S(1)}, u32[]{:S(2)}, u32[]{:S(2)}) collective-permute-start(f32[34,16,128]{2,1,0:T(8,128)S(1)} %get-tuple-element.57), channel_id=1, source_target_pairs={{0,8},{1,9},{2,10},{3,11},{4,12},{5,13},{6,14},{7,15},{8,0},{9,1},... | collective-permute-start | bytes 835592 | tf_op jit(solution)/shard_map/ppermute | solution.py:246
  68.6 1.6 %collective-permute-start.12 = (bf16[34,16,128]{2,1,0:T(8,128)(2,1)S(1)}, bf16[34,16,128]{2,1,0:T(8,128)(2,1)S(1)}, u32[]{:S(2)}, u32[]{:S(2)}) collective-permute-start(bf16[34,16,128]{2,1,0:T(8,128)(2,1)S(1)} %get-tuple-element.58), channel_id=1, source_target_pairs={{0,8},{1,9},{2,10},{3,11},{4,12},{5,13},{6,14},{7,15},{8,0},{9,1},... | collective-permute-start | bytes 417800 | tf_op jit(solution)/shard_map/ppermute | solution.py:246
  70.2 6.4 %collective-permute-done.5.two = bf16[68,16,128]{2,1,0:T(8,128)(2,1)S(1)} collective-permute-done((bf16[68,16,128]{2,1,0:T(8,128)(2,1)S(1)}, bf16[68,16,128]{2,1,0:T(8,128)(2,1)S(1)}, u32[]{:S(2)}, u32[]{:S(2)}) %collective-permute-start.5) | collective-permute-done | bytes 278560 | tf_op jit(solution)/shard_map/ppermute | solution.py:246
  76.6 0.0 collective-permute-done.6.three
  76.6 0.7 collective-permute-done.7.four
  77.3 0.8 collective-permute-done.12.imag_ref
  78.1 0.0 collective-permute-done.11.real_ref
  78.1 0.7 shard_map.89
  78.8 2.8 %collective-permute-start.13 = (f32[272,128]{1,0:T(8,128)S(1)}, f32[272,128]{1,0:T(8,128)S(1)}, u32[]{:S(2)}, u32[]{:S(2)}) collective-permute-start(f32[272,128]{1,0:T(8,128)S(1)} %get-tuple-element.60), channel_id=1, source_target_pairs={{0,2},{1,3},{2,0},{3,1},{4,6},{5,7},{6,4},{7,5},{8,10},{9,11},{10,... | collective-permute-start | bytes 417800 | tf_op jit(solution)/shard_map/ppermute | solution.py:246
  81.6 0.8 collective-permute-start.14
  82.5 2.4 %collective-permute-start.15 = (f32[272,128]{1,0:T(8,128)S(1)}, f32[272,128]{1,0:T(8,128)S(1)}, u32[]{:S(2)}, u32[]{:S(2)}) collective-permute-start(f32[272,128]{1,0:T(8,128)S(1)} %get-tuple-element.62), channel_id=1, source_target_pairs={{0,66},{1,67},{2,64},{3,65},{4,70},{5,71},{6,68},{7,69},{8,74},{9,... | collective-permute-start | bytes 417800 | tf_op jit(solution)/shard_map/ppermute | solution.py:246
  84.9 1.5 %collective-permute-done.13.refs_1_ = f32[272,128]{1,0:T(8,128)S(1)} collective-permute-done((f32[272,128]{1,0:T(8,128)S(1)}, f32[272,128]{1,0:T(8,128)S(1)}, u32[]{:S(2)}, u32[]{:S(2)}) %collective-permute-start.13) | collective-permute-done | bytes 139296 | tf_op jit(solution)/shard_map/ppermute | solution.py:246
  86.4 1.8 %collective-permute-done.14.refs_2_ = f32[272,128]{1,0:T(8,128)S(1)} collective-permute-done((f32[272,128]{1,0:T(8,128)S(1)}, f32[272,128]{1,0:T(8,128)S(1)}, u32[]{:S(2)}, u32[]{:S(2)}) %collective-permute-start.14) | collective-permute-done | bytes 139296 | tf_op jit(solution)/shard_map/ppermute | solution.py:246
  88.2 0.0 collective-permute-done.15.refs_3_
  88.2 0.0 copy-done
  88.2 1.0 %shard_map.90 = f32[17,2048]{1,0:T(8,128)} custom-call(f32[272,128]{1,0:T(8,128)S(1)} %get-tuple-element.59.refs_0_, f32[272,128]{1,0:T(8,128)S(1)} %collective-permute-done.13.refs_1_, f32[272,128]{1,0:T(8,128)S(1)} %collective-permute-done.14.refs_2_, f32[272,128]{1,0:T(8,128)S(1)} %collective-permute-done.15.refs_3_, f32[128,128]{1,0:T(8,128)S(1)} %copy-done), custom_call_target="tpu_custom_call" | custom-call | tf_op jit(solution)/shard_map/pallas_call | solution.py:336
  (12 shorter events, 0.1 us)
Async XLA Ops:
  3.0 20.6 %all-to-all-start = ((bf16[8,528,128]{2,1,0:T(8,128)(2,1)}), bf16[8,528,128]{2,1,0:T(8,128)(2,1)S(1)}, u32[]{:S(2)}, u32[]{:S(2)}) async-start(bf16[8,528,128]{2,1,0:T(8,128)(2,1)} %shard_map.82), calls=%async_computation | async-start | bytes 2162688 | tf_op jit(solution)/shard_map/all_to_all | solution.py:272
  23.7 5.3 %collective-permute-start = (bf16[8,528,128]{2,1,0:T(8,128)(2,1)S(1)}, bf16[8,528,128]{2,1,0:T(8,128)(2,1)S(1)}, u32[]{:S(2)}, u32[]{:S(2)}) collective-permute-start(bf16[8,528,128]{2,1,0:T(8,128)(2,1)S(1)} %all-to-all-done.refs_3_), channel_id=1, source_target_pairs={{0,1},{1,0},{2,3},{3,2},{4,5},{5,4},{6,7},{7,6},{8,9},{9,8},{10,11... | collective-permute-start | bytes 3244040 | tf_op jit(solution)/shard_map/ppermute | solution.py:246
  24.1 5.1 %copy-start.2 = (f32[4]{0:T(128)S(1)}, f32[4]{0:T(128)}, u32[]{:S(2)}) copy-start(f32[4]{0:T(128)} %param.13) | copy-start | bytes 52
  24.1 5.7 %copy-start.1 = (f32[3,512]{1,0:T(4,128)S(1)}, f32[3,512]{1,0:T(4,128)}, u32[]{:S(2)}) copy-start(f32[3,512]{1,0:T(4,128)} %param.12) | copy-start | bytes 18436
  25.2 12.4 %collective-permute-start.2 = (bf16[4,528,128]{2,1,0:T(8,128)(2,1)}, bf16[4,528,128]{2,1,0:T(8,128)(2,1)S(1)}, u32[]{:S(2)}, u32[]{:S(2)}) collective-permute-start(bf16[4,528,128]{2,1,0:T(8,128)(2,1)} %get-tuple-element.63), channel_id=1, source_target_pairs={{0,4},{1,13},{2,6},{3,15},{4,8},{5,1},{6,10},{7,3},{8,12},{9,5},{1... | collective-permute-start | bytes 1622024 | tf_op jit(solution)/shard_map/ppermute | solution.py:246
  27.1 15.5 %collective-permute-start.1 = (bf16[4,528,128]{2,1,0:T(8,128)(2,1)}, bf16[4,528,128]{2,1,0:T(8,128)(2,1)S(1)}, u32[]{:S(2)}, u32[]{:S(2)}) collective-permute-start(bf16[4,528,128]{2,1,0:T(8,128)(2,1)} %get-tuple-element.64), channel_id=1, source_target_pairs={{0,4},{1,13},{2,6},{3,15},{4,8},{5,1},{6,10},{7,3},{8,12},{9,5},{1... | collective-permute-start | bytes 1622024 | tf_op jit(solution)/shard_map/ppermute | solution.py:246
  42.5 3.2 %collective-permute-start.3 = (bf16[4,528,128]{2,1,0:T(8,128)(2,1)S(1)}, bf16[4,528,128]{2,1,0:T(8,128)(2,1)S(1)}, u32[]{:S(2)}, u32[]{:S(2)}) collective-permute-start(bf16[4,528,128]{2,1,0:T(8,128)(2,1)S(1)} %collective-permute-done.1.refs_3_.refs_4_), channel_id=1, source_target_pairs={{0,1},{1,0},{2,3},{3,2},{4,5},{5,4},{6,7},{7,6},{8,9},{9,8},{10,11... | collective-permute-start | bytes 1622024 | tf_op jit(solution)/shard_map/ppermute | solution.py:246
  42.5 3.2 %collective-permute-start.4 = (bf16[4,528,128]{2,1,0:T(8,128)(2,1)S(1)}, bf16[4,528,128]{2,1,0:T(8,128)(2,1)S(1)}, u32[]{:S(2)}, u32[]{:S(2)}) collective-permute-start(bf16[4,528,128]{2,1,0:T(8,128)(2,1)S(1)} %collective-permute-done.2.refs_4_.refs_5_), channel_id=1, source_target_pairs={{0,1},{1,0},{2,3},{3,2},{4,5},{5,4},{6,7},{7,6},{8,9},{9,8},{10,11... | collective-permute-start | bytes 1622024 | tf_op jit(solution)/shard_map/ppermute | solution.py:246
  48.8 15.4 %collective-permute-start.8 = (bf16[68,16,128]{2,1,0:T(8,128)(2,1)S(1)}, bf16[68,16,128]{2,1,0:T(8,128)(2,1)S(1)}, u32[]{:S(2)}, u32[]{:S(2)}) collective-permute-start(bf16[68,16,128]{2,1,0:T(8,128)(2,1)S(1)} %get-tuple-element.54), channel_id=1, source_target_pairs={{0,16},{1,17},{2,18},{3,19},{4,20},{5,21},{6,22},{7,23},{8,24},{9,... | collective-permute-start | bytes 835592 | tf_op jit(solution)/shard_map/ppermute | solution.py:246
  49.7 15.6 %collective-permute-start.9 = (bf16[68,16,128]{2,1,0:T(8,128)(2,1)S(1)}, bf16[68,16,128]{2,1,0:T(8,128)(2,1)S(1)}, u32[]{:S(2)}, u32[]{:S(2)}) collective-permute-start(bf16[68,16,128]{2,1,0:T(8,128)(2,1)S(1)} %get-tuple-element.55), channel_id=1, source_target_pairs={{0,32},{1,33},{2,34},{3,35},{4,36},{5,37},{6,38},{7,39},{8,40},{9,... | collective-permute-start | bytes 835592 | tf_op jit(solution)/shard_map/ppermute | solution.py:246
  51.8 14.7 %collective-permute-start.10 = (bf16[68,16,128]{2,1,0:T(8,128)(2,1)S(1)}, bf16[68,16,128]{2,1,0:T(8,128)(2,1)S(1)}, u32[]{:S(2)}, u32[]{:S(2)}) collective-permute-start(bf16[68,16,128]{2,1,0:T(8,128)(2,1)S(1)} %get-tuple-element.56), channel_id=1, source_target_pairs={{0,48},{1,49},{2,50},{3,51},{4,52},{5,53},{6,54},{7,55},{8,56},{9,... | collective-permute-start | bytes 835592 | tf_op jit(solution)/shard_map/ppermute | solution.py:246
  57.7 18.9 %collective-permute-start.5 = (bf16[68,16,128]{2,1,0:T(8,128)(2,1)S(1)}, bf16[68,16,128]{2,1,0:T(8,128)(2,1)S(1)}, u32[]{:S(2)}, u32[]{:S(2)}) collective-permute-start(bf16[68,16,128]{2,1,0:T(8,128)(2,1)S(1)} %get-tuple-element.50), channel_id=1, source_target_pairs={{0,16},{1,17},{2,18},{3,19},{4,20},{5,21},{6,22},{7,23},{8,24},{9,... | collective-permute-start | bytes 835592 | tf_op jit(solution)/shard_map/ppermute | solution.py:246
  58.3 18.3 %collective-permute-start.6 = (bf16[68,16,128]{2,1,0:T(8,128)(2,1)S(1)}, bf16[68,16,128]{2,1,0:T(8,128)(2,1)S(1)}, u32[]{:S(2)}, u32[]{:S(2)}) collective-permute-start(bf16[68,16,128]{2,1,0:T(8,128)(2,1)S(1)} %get-tuple-element.51), channel_id=1, source_target_pairs={{0,32},{1,33},{2,34},{3,35},{4,36},{5,37},{6,38},{7,39},{8,40},{9,... | collective-permute-start | bytes 835592 | tf_op jit(solution)/shard_map/ppermute | solution.py:246
  64.2 24.0 %copy-start = (f32[128,128]{1,0:T(8,128)S(1)}, f32[128,128]{1,0:T(8,128)}, u32[]{:S(2)}) copy-start(f32[128,128]{1,0:T(8,128)} %constant.111.clone.refs_4_) | copy-start | bytes 196612
  64.2 13.1 %collective-permute-start.7 = (bf16[68,16,128]{2,1,0:T(8,128)(2,1)S(1)}, bf16[68,16,128]{2,1,0:T(8,128)(2,1)S(1)}, u32[]{:S(2)}, u32[]{:S(2)}) collective-permute-start(bf16[68,16,128]{2,1,0:T(8,128)(2,1)S(1)} %get-tuple-element.52), channel_id=1, source_target_pairs={{0,48},{1,49},{2,50},{3,51},{4,52},{5,53},{6,54},{7,55},{8,56},{9,... | collective-permute-start | bytes 835592 | tf_op jit(solution)/shard_map/ppermute | solution.py:246
  66.6 11.5 %collective-permute-start.11 = (f32[34,16,128]{2,1,0:T(8,128)S(1)}, f32[34,16,128]{2,1,0:T(8,128)S(1)}, u32[]{:S(2)}, u32[]{:S(2)}) collective-permute-start(f32[34,16,128]{2,1,0:T(8,128)S(1)} %get-tuple-element.57), channel_id=1, source_target_pairs={{0,8},{1,9},{2,10},{3,11},{4,12},{5,13},{6,14},{7,15},{8,0},{9,1},... | collective-permute-start | bytes 835592 | tf_op jit(solution)/shard_map/ppermute | solution.py:246
  68.6 9.5 %collective-permute-start.12 = (bf16[34,16,128]{2,1,0:T(8,128)(2,1)S(1)}, bf16[34,16,128]{2,1,0:T(8,128)(2,1)S(1)}, u32[]{:S(2)}, u32[]{:S(2)}) collective-permute-start(bf16[34,16,128]{2,1,0:T(8,128)(2,1)S(1)} %get-tuple-element.58), channel_id=1, source_target_pairs={{0,8},{1,9},{2,10},{3,11},{4,12},{5,13},{6,14},{7,15},{8,0},{9,1},... | collective-permute-start | bytes 417800 | tf_op jit(solution)/shard_map/ppermute | solution.py:246
  78.8 7.5 %collective-permute-start.13 = (f32[272,128]{1,0:T(8,128)S(1)}, f32[272,128]{1,0:T(8,128)S(1)}, u32[]{:S(2)}, u32[]{:S(2)}) collective-permute-start(f32[272,128]{1,0:T(8,128)S(1)} %get-tuple-element.60), channel_id=1, source_target_pairs={{0,2},{1,3},{2,0},{3,1},{4,6},{5,7},{6,4},{7,5},{8,10},{9,11},{10,... | collective-permute-start | bytes 417800 | tf_op jit(solution)/shard_map/ppermute | solution.py:246
  81.6 6.6 %collective-permute-start.14 = (f32[272,128]{1,0:T(8,128)S(1)}, f32[272,128]{1,0:T(8,128)S(1)}, u32[]{:S(2)}, u32[]{:S(2)}) collective-permute-start(f32[272,128]{1,0:T(8,128)S(1)} %get-tuple-element.61), channel_id=1, source_target_pairs={{0,64},{1,65},{2,66},{3,67},{4,68},{5,69},{6,70},{7,71},{8,72},{9,... | collective-permute-start | bytes 417800 | tf_op jit(solution)/shard_map/ppermute | solution.py:246
  82.5 5.7 %collective-permute-start.15 = (f32[272,128]{1,0:T(8,128)S(1)}, f32[272,128]{1,0:T(8,128)S(1)}, u32[]{:S(2)}, u32[]{:S(2)}) collective-permute-start(f32[272,128]{1,0:T(8,128)S(1)} %get-tuple-element.62), channel_id=1, source_target_pairs={{0,66},{1,67},{2,64},{3,65},{4,70},{5,71},{6,68},{7,69},{8,74},{9,... | collective-permute-start | bytes 417800 | tf_op jit(solution)/shard_map/ppermute | solution.py:246
